TPU v7x, 32 devices: a whole 2x2x4 slice. The times are simulated.
32 devices in a mesh: grp: 2 (over x), node: 16 (over z, y, core).
Axes of the slice: x: 2, y: 2, z: 4, core: 2. Of those that a mesh axis runs over, the one named last changes fastest.
Arguments:
- nodes: bfloat16 [128, 2, 1024, 1024], P('grp', None, 'node'), parts along dimension 0, may hold values from -0.34960938 to 0.34960938
- pair_nodes: int32 [16, 2], replicated, may hold values from 0 to 63
- prod_left: int32 [16], replicated, may hold values from 0 to 15, as said below
- prod_right: int32 [16], replicated, may hold values from 0 to 15, each once
- prod_flag: int32 [16], replicated, may hold values from 0 to 1
- prod_diag: int32 [16], replicated, may hold values from 0 to 7, as said below
Outputs:
- diagrams: bfloat16 [16, 2, 1024, 1024], P('grp', None, 'node'), parts along dimension 0
There are 2 independent parts, one for each index of `grp`. A program takes and returns all parts, laid end to end along the dimension named above; an argument that names none is the same for every part. Nothing has to cross between parts.
Inputs may be any that keep to these rules, and one draw needn't show every extreme that they name: `prod_left`: exactly 8 distinct pairs are left operands, each of exactly two products. `prod_diag`: every diagram receives exactly two products.
All inputs are finite; a program needn't handle non-finite values.
Results may differ from a plain program's by a relative error of at most 0.0065.
Values may be sent and summed in bfloat16 or wider, within the bound.
No kernel may reach another device: no remote copies, remote signals or barrier semaphores. Data moves between devices by JAX's collectives and lax.ppermute only.
A program may use at most 128 MiB of HBM per device.

v0:
```python
import functools

import jax
import jax.numpy as jnp
from jax import lax
from jax.experimental import pallas as pl
from jax.experimental.pallas import tpu as pltpu
from jax.sharding import PartitionSpec as P

SHARES = (1, 1)
SET = 4
BLOCKS = 4
VMEM_BYTES = 48 * 1024 * 1024
PANELS_VMEM_BYTES = 56 * 1024 * 1024
WHOLE_VMEM_BYTES = 60 * 1024 * 1024
SMEM = pl.BlockSpec(memory_space=pltpu.SMEM)
HBM = pl.BlockSpec(memory_space=pltpu.HBM)
VMEM = pl.BlockSpec(memory_space=pltpu.VMEM)


def params(limit=VMEM_BYTES):
    return pltpu.CompilerParams(vmem_limit_bytes=limit)


def route_kernel(
    prods, place_ref, pair_nodes, prod_left, prod_right, prod_flag, prod_diag, table, by_left, diag, mate, seen, kind, slots
):
    diags = prods // 2
    mine = place_ref[0] // SET

    def clear(k, carry):
        mate[k] = 0
        seen[k] = 0
        slots[k] = 0
        table[4, k] = -1
        table[5, k] = -1
        table[6, k] = 0
        table[7, k] = -1
        table[8, k] = 0
        return carry

    lax.fori_loop(0, prods, clear, 0)

    def rank(k, carry):
        own = prod_left[k]

        def count(j, total):
            other = prod_left[j]
            before = jnp.logical_or(other < own, jnp.logical_and(other == own, j < k))
            return total + before.astype(jnp.int32)

        at = lax.fori_loop(0, prods, count, 0, unroll=True)
        by_left[at] = k
        diag[at] = prod_diag[k]
        return carry

    lax.fori_loop(0, prods, rank, 0)

    def pair_up(s, carry):
        own = diag[s]

        def find(j, found):
            same = jnp.logical_and(diag[j] == own, j != s)
            return jnp.where(same, j, found)

        mate[s] = lax.fori_loop(0, prods, find, s, unroll=True)
        return carry

    lax.fori_loop(0, prods, pair_up, 0)

    def sibling_of(s):
        return s + 1 - 2 * lax.rem(s, 2)

    def kind_of(g, carry):
        def step(_, state):
            s, length = state
            back = s // 2 == g
            return jnp.where(back, s, mate[sibling_of(s)]), jnp.where(back, length, length + 1)

        _, length = lax.fori_loop(0, diags, step, (mate[2 * g + 1], 1))
        kind[g] = jnp.where(lax.rem(length, 2) == 0, 0, jnp.where(length == 1, 2, 1))
        return carry

    lax.fori_loop(0, diags, kind_of, 0)

    def add(device, s):
        k = by_left[s]
        right = prod_right[k]
        table[0, device] = pair_nodes[prod_left[k], lax.rem(device, 2)]
        table[1, device] = pair_nodes[right, 0]
        table[2, device] = pair_nodes[right, 1]
        table[3, device] = prod_flag[k]
        d = diag[s]
        owner = device // SET
        code = SET * jnp.bitwise_xor(owner, mine)
        earlier = table[4, d]
        shared = jnp.logical_and(earlier >= 0, earlier // SET == code // SET)
        slot = jnp.where(shared, earlier - code, slots[owner])

        @pl.when(jnp.logical_not(shared))
        def _():
            slots[owner] = slot + 1
            table[8, 0] = jnp.maximum(table[8, 0], slot + 1)
            table[jnp.where(earlier >= 0, 5, 4), d] = code + slot

        @pl.when(owner == mine)
        def _():
            table[jnp.where(shared, 7, 6), slot] = lax.rem(device, SET)

    def walk(n, carry):
        s, last = carry

        def first(j, found):
            g = diags - 1 - j
            own = kind[g]
            worth = jnp.where(own == 0, 3, jnp.where(own == last, 1, 2))
            worth = jnp.where(seen[g] == 0, worth, 0)
            best, at = found
            return jnp.maximum(best, worth), jnp.where(worth >= best, g, at)

        _, fresh = lax.fori_loop(0, diags, first, (1, 0), unroll=True)
        s = jnp.where(seen[s // 2] == 0, s, 2 * fresh)
        seen[s // 2] = 1
        add(2 * n, s)
        add(2 * n + 1, sibling_of(s))
        return mate[sibling_of(s)], kind[s // 2]

    lax.fori_loop(0, diags, walk, (0, 2))


def route(place, pair_nodes, prod_left, prod_right, prod_flag, prod_diag):
    prods = prod_left.shape[0]
    return pl.pallas_call(
        functools.partial(route_kernel, prods),
        out_shape=jax.ShapeDtypeStruct((9, prods), jnp.int32),
        in_specs=[SMEM] * 6,
        out_specs=SMEM,
        scratch_shapes=[pltpu.SMEM((prods,), jnp.int32)] * 6,
        name="route",
    )(place, pair_nodes, prod_left, prod_right, prod_flag, prod_diag)


def pick_kernel(row, start, table, nodes, out, held, reads, writes):
    count, _, _, width = out.shape

    def read(t):
        node = nodes.at[table[row, t], :, :, pl.ds(start, width)]
        return pltpu.make_async_copy(node, held.at[t], reads.at[t])

    def write(t):
        return pltpu.make_async_copy(held.at[t], out.at[t], writes.at[t])

    for t in range(count):
        read(t).start()
    for t in range(count):
        read(t).wait()
        write(t).start()
    for t in range(count):
        write(t).wait()


def pick(table, nodes, row, start, width):
    count = table.shape[1]
    shape = (count, nodes.shape[1], nodes.shape[2], width)
    return pl.pallas_call(
        functools.partial(pick_kernel, row, start),
        out_shape=jax.ShapeDtypeStruct(shape, nodes.dtype),
        in_specs=[SMEM, HBM],
        out_specs=HBM,
        scratch_shapes=[
            pltpu.VMEM(shape, nodes.dtype),
            pltpu.SemaphoreType.DMA((count,)),
            pltpu.SemaphoreType.DMA((count,)),
        ],
        compiler_params=params(WHOLE_VMEM_BYTES),
        name="pick",
    )(table, nodes)


def dot(a, b):
    return jnp.dot(a, b, preferred_element_type=jnp.float32)


def left_kernel(table, place, own, other, out, left, right, sems):
    order = left.shape[2] * left.shape[0]
    core = lax.rem(place[0], 2)
    flag = table[3, place[0]]

    def load(first, second):
        one = pltpu.make_async_copy(first, left, sems.at[0])
        two = pltpu.make_async_copy(second, right, sems.at[1])
        one.start()
        two.start()
        one.wait()
        two.wait()

    @pl.when(core == 0)
    def _():
        load(own, other)

    @pl.when(core == 1)
    def _():
        load(other, own)

    b_re = right[:, 0].reshape(order, order)
    b_im = right[:, 1].reshape(order, order)
    step = order // 4
    per = left.shape[0] // 4
    for block in range(4):
        a_re = left[block * per : (block + 1) * per, 0].reshape(step, order)
        a_im = left[block * per : (block + 1) * per, 1].reshape(step, order)
        re = (dot(a_re, b_re) - dot(a_im, b_im)).astype(out.dtype)
        im = (dot(a_re, b_im) + dot(a_im, b_re)).astype(out.dtype)

        @pl.when(flag == 0)
        def _():
            out[0, block * step : (block + 1) * step, :] = re
            out[1, block * step : (block + 1) * step, :] = im

        @pl.when(flag == 1)
        def _():
            out[0, :, block * step : (block + 1) * step] = re.T
            out[1, :, block * step : (block + 1) * step] = -im.T


def left_pair(table, place, own, other):
    order = other.shape[3]
    return pl.pallas_call(
        left_kernel,
        out_shape=jax.ShapeDtypeStruct((2, order, order), own.dtype),
        in_specs=[SMEM, SMEM, HBM, HBM],
        out_specs=VMEM,
        scratch_shapes=[
            pltpu.VMEM(other.shape, other.dtype),
            pltpu.VMEM(other.shape, other.dtype),
            pltpu.SemaphoreType.DMA((2,)),
        ],
        compiler_params=params(),
        name="left_pair",
    )(table, place, own, other)


def product_kernel(left, right, out):
    order = left.shape[2]
    b_re = right[:, 0].reshape(order, order)
    b_im = right[:, 1].reshape(order, order)
    step = order // BLOCKS
    for block in range(BLOCKS):
        rows = slice(block * step, (block + 1) * step)
        a_re = left[0, rows, :]
        a_im = left[1, rows, :]
        out[0, rows, :] = (dot(a_re, b_re) - dot(a_im, b_im)).astype(out.dtype)
        out[1, rows, :] = (dot(a_re, b_im) + dot(a_im, b_re)).astype(out.dtype)


def product(left, right):
    order = left.shape[2]
    return pl.pallas_call(
        product_kernel,
        out_shape=jax.ShapeDtypeStruct(left.shape, left.dtype),
        in_specs=[VMEM, VMEM],
        out_specs=VMEM,
        compiler_params=params(),
        name="product",
    )(left, right)


def panels_kernel(place, left_hbm, right_hbm, *refs):
    outs, (left, right, scratch, sems) = refs[:-4], refs[-4:]
    order = left.shape[2]
    width = right.shape[3]
    rows_each = right.shape[2]
    step = order // BLOCKS
    per = step // rows_each
    own = lax.rem(place[0], SET)
    copies = [pltpu.make_async_copy(right_hbm, right, sems.at[BLOCKS])]
    for block in range(BLOCKS):
        rows = slice(block * step, (block + 1) * step)
        copies.append(pltpu.make_async_copy(left_hbm.at[:, rows], left.at[:, rows], sems.at[block]))
    for copy in copies:
        copy.start()
    copies[0].wait()
    b_re = right[:, 0].reshape(order, width)
    b_im = right[:, 1].reshape(order, width)
    for block in range(BLOCKS):
        copies[block + 1].wait()
        rows = slice(block * step, (block + 1) * step)
        a_re = left[0, rows, :]
        a_im = left[1, rows, :]
        re = (dot(a_re, b_re) - dot(a_im, b_im)).astype(scratch.dtype)
        im = (dot(a_re, b_im) + dot(a_im, b_re)).astype(scratch.dtype)
        panels = slice(block * per, (block + 1) * per)
        scratch[panels, 0] = re.reshape(per, rows_each, width)
        scratch[panels, 1] = im.reshape(per, rows_each, width)
    for s, out in enumerate(outs):
        target = jnp.bitwise_xor(own, s)
        for owner in range(out.shape[0]):
            out[owner] = scratch[SET * owner + target]


def panels_of(place, left, right):
    count, two, rows, width = right.shape
    return pl.pallas_call(
        panels_kernel,
        out_shape=[jax.ShapeDtypeStruct((count // SET, two, rows, width), left.dtype)] * SET,
        in_specs=[SMEM, HBM, HBM],
        out_specs=[VMEM] * SET,
        scratch_shapes=[
            pltpu.VMEM(left.shape, left.dtype),
            pltpu.VMEM(right.shape, right.dtype),
            pltpu.VMEM(right.shape, right.dtype),
            pltpu.SemaphoreType.DMA((BLOCKS + 1,)),
        ],
        compiler_params=params(PANELS_VMEM_BYTES),
        name="panels",
    )(place, left, right)


def partial_kernel(table, place, *refs):
    pieces, outs, scratch = refs[:SET], refs[SET:-1], refs[-1]
    own = lax.rem(place[0], SET)
    mine = place[0] // SET
    for s, piece in enumerate(pieces):
        scratch[s] = piece[...]
    for slot in range(outs[0].shape[0]):
        one = jnp.bitwise_xor(table[6, slot], own)
        second = table[7, slot]
        two = jnp.bitwise_xor(jnp.maximum(second, 0), own)
        for e, out in enumerate(outs):
            owner = jnp.bitwise_xor(mine, e)
            other = scratch[two, owner].astype(jnp.float32)
            total = scratch[one, owner].astype(jnp.float32) + jnp.where(second >= 0, other, 0.0)
            out[slot] = total.astype(out.dtype)


def partial_sums(slots, table, place, pieces):
    sets = pieces[0].shape[0]
    shape = pieces[0].shape[1:]
    return pl.pallas_call(
        partial_kernel,
        out_shape=[jax.ShapeDtypeStruct((slots,) + shape, pieces[0].dtype)] * sets,
        in_specs=[SMEM, SMEM] + [VMEM] * SET,
        out_specs=[VMEM] * sets,
        scratch_shapes=[pltpu.VMEM((SET,) + pieces[0].shape, pieces[0].dtype)],
        compiler_params=params(),
        name="partial_sums",
    )(table, place, *pieces)


def diagrams_kernel(parts, sets, table, *refs):
    ins, out, held = refs[: parts * sets], refs[parts * sets], refs[parts * sets + 1]

    start = 0
    for j in range(parts):
        width = ins[j * sets].shape[3]
        for e in range(sets):
            held[e, :, :, :, start : start + width] = ins[j * sets + e][...]
        start += width

    for d in range(out.shape[0]):
        one, two = table[4, d], jnp.maximum(table[5, d], 0)
        first = held[one // SET, lax.rem(one, SET)].astype(jnp.float32)
        second = held[two // SET, lax.rem(two, SET)].astype(jnp.float32)
        out[d] = (first + jnp.where(table[5, d] >= 0, second, 0.0)).astype(out.dtype)


def diagrams_of(table, parts):
    slots, two, rows, _ = parts[0][0].shape
    sets = len(parts[0])
    diags = table.shape[1] // 2
    whole = sum(pieces[0].shape[3] for pieces in parts)
    dtype = parts[0][0].dtype
    return pl.pallas_call(
        functools.partial(diagrams_kernel, len(parts), sets),
        out_shape=jax.ShapeDtypeStruct((diags, two, rows, whole), dtype),
        in_specs=[SMEM] + [VMEM] * (sets * len(parts)),
        out_specs=VMEM,
        scratch_shapes=[pltpu.VMEM((sets, slots, two, rows, whole), dtype)],
        compiler_params=params(),
        name="diagrams",
    )(table, *[x for pieces in parts for x in pieces])


def exchange(x):
    return lax.all_to_all(x, "node", split_axis=0, concat_axis=0, tiled=True)


def after(x, earlier):
    return lax.optimization_barrier((x, earlier))[0]


def swap(x, size, shift):
    return lax.ppermute(x, "node", [(i, i ^ shift) for i in range(size)])


def tail(slots, size, table, place, picks, left, middle):
    left_middle = product(left, middle)
    done = middle
    parts = []
    for picked in picks:
        last = exchange(after(picked, done))
        if parts:
            last = after(last, parts[-1][0])
        sent = panels_of(place, left_middle, last)
        pieces = [sent[0]] + [swap(sent[s], size, s) for s in range(1, SET)]
        sums = partial_sums(slots, table, place, pieces)
        done = (last, left_middle)
        parts.append([sums[0]] + [swap(x, size, SET * e) for e, x in enumerate(sums) if e])
    return diagrams_of(table, parts)


def local(size, nodes, pair_nodes, prod_left, prod_right, prod_flag, prod_diag):
    place = lax.axis_index("node").astype(jnp.int32).reshape(1)
    order = nodes.shape[3]
    table = route(place, pair_nodes, prod_left, prod_right, prod_flag, prod_diag)
    own = exchange(pick(table, nodes, 0, 0, order))
    other = swap(own, size, 1)
    middle = exchange(after(pick(table, nodes, 1, 0, order), own))
    left = left_pair(table, place, own, other)
    widths = [order * share // sum(SHARES) for share in SHARES]
    picks = [pick(table, nodes, 2, sum(widths[:j]), width) for j, width in enumerate(widths)]
    few = functools.partial(tail, SET - 1, size)
    many = functools.partial(tail, SET, size)
    return lax.cond(table[8, 0] < SET, few, many, table, place, picks, left, middle)


def solution(mesh):
    placed = (P("grp", None, "node", None), P(), P(), P(), P(), P())
    return jax.shard_map(
        functools.partial(local, mesh.shape["node"]),
        mesh=mesh,
        in_specs=placed,
        out_specs=P("grp", None, "node", None),
        check_vma=False,
    )
```

profile of v0, /device:TPU:10, one launch (start us, length us, event | category | flops | bytes accessed | tf_op | source)
XLA Modules:
  0.0 399.7 jit_solution(6083953151335656991)
XLA Ops:
  1.4 4.6 %route.1.table = s32[9,16]{1,0:T(8,128)S(1)} custom-call(s32[1]{0:T(128)} %bitcast.place_ref.place, s32[16,2]{1,0:T(8,128)} %copy.9.pair_nodes, s32[16]{0:T(128)} %prod_left.1, s32[16]{0:T(128)} %prod_right.1, s32[16]{0:T(128)} %prod_flag.1, s32[16]{0:T(128)} %prod_diag.1), custom_call_target="tpu_custom_call" | custom-call | tf_op jit(solution)/shard_map/route/pallas_call | solution.py:133
  5.9 4.5 %pick.4 = bf16[16,2,64,1024]{3,2,1,0:T(8,128)(2,1)} custom-call(s32[9,16]{1,0:T(8,128)S(1)} %route.1.table, bf16[64,2,64,1024]{3,2,1,0:T(8,128)(2,1)} %nodes.7), custom_call_target="tpu_custom_call" | custom-call | tf_op jit(solution)/shard_map/pick/pallas_call | solution.py:165
  10.5 6.3 %all-to-all-start.4 = ((bf16[16,2,64,1024]{3,2,1,0:T(8,128)(2,1)}), bf16[16,2,64,1024]{3,2,1,0:T(8,128)(2,1)}, u32[]{:S(2)}, u32[]{:S(2)}) async-start(bf16[16,2,64,1024]{3,2,1,0:T(8,128)(2,1)} %pick.4), calls=%async_computation.4 | async-start | bytes 8388608 | tf_op jit(solution)/shard_map/all_to_all | solution.py:385
  16.8 5.0 %pick.5 = bf16[16,2,64,1024]{3,2,1,0:T(8,128)(2,1)} custom-call(s32[9,16]{1,0:T(8,128)S(1)} %route.1.table, bf16[64,2,64,1024]{3,2,1,0:T(8,128)(2,1)} %nodes.7), custom_call_target="tpu_custom_call" | custom-call | tf_op jit(solution)/shard_map/pick/pallas_call | solution.py:165
  21.8 85.8 %all-to-all-done.4.own = bf16[16,2,64,1024]{3,2,1,0:T(8,128)(2,1)} async-done(((bf16[16,2,64,1024]{3,2,1,0:T(8,128)(2,1)}), bf16[16,2,64,1024]{3,2,1,0:T(8,128)(2,1)}, u32[]{:S(2)}, u32[]{:S(2)}) %all-to-all-start.4) | async-done | bytes 4194336 | tf_op jit(solution)/shard_map/all_to_all | solution.py:385
  107.6 6.6 %all-to-all-start.5 = ((bf16[16,2,64,1024]{3,2,1,0:T(8,128)(2,1)}), bf16[16,2,64,1024]{3,2,1,0:T(8,128)(2,1)}, u32[]{:S(2)}, u32[]{:S(2)}) async-start(bf16[16,2,64,1024]{3,2,1,0:T(8,128)(2,1)} %pick.5), calls=%async_computation.5 | async-start | bytes 8388608 | tf_op jit(solution)/shard_map/all_to_all | solution.py:385
  114.8 3.3 pick.7
  118.1 3.2 pick.6
  122.0 16.9 %left_pair.1 = bf16[2,1024,1024]{2,1,0:T(8,128)(2,1)} custom-call(s32[9,16]{1,0:T(8,128)S(1)} %route.1.table, s32[1]{0:T(128)} %bitcast.place_ref.place, bf16[16,2,64,1024]{3,2,1,0:T(8,128)(2,1)} %all-to-all-done.4.own, bf16[16,2,64,1024]{3,2,1,0:T(8,128)(2,1)} %collective-permute-done.24.other), custom_call_target="tpu_custom_call" | custom-call | tf_op jit(solution)/shard_map/left_pair/pallas_call | solution.py:228
  138.9 66.1 %all-to-all-done.5 = bf16[16,2,64,1024]{3,2,1,0:T(8,128)(2,1)} async-done(((bf16[16,2,64,1024]{3,2,1,0:T(8,128)(2,1)}), bf16[16,2,64,1024]{3,2,1,0:T(8,128)(2,1)}, u32[]{:S(2)}, u32[]{:S(2)}) %all-to-all-start.5) | async-done | bytes 4194336 | tf_op jit(solution)/shard_map/all_to_all | solution.py:385
  205.0 193.4 %conditional.1 = (bf16[8,2,64,1024]{3,2,1,0:T(8,128)(2,1)S(1)}) conditional(s32[]{:T(128)} %bitcast.1, (bf16[2,1024,1024]{2,1,0:T(8,128)(2,1)}, bf16[16,2,64,1024]{3,2,1,0:T(8,128)(2,1)}, bf16[16,2,64,512]{3,2,1,0:T(8,128)(2,1)}, s32[1]{0:T(128)}, s32[9,16]{1,0:T(8,128)S(1)}, /*index=5*/bf16[16,2,64,512]{3,2,1,0:T(8,128)(2,1)}) %tuple.19, ...), branch_computations={%region_0.0_spmd, %region_1.0_spmd} | conditional | bytes 67109528 | solution.py:424
  205.0 6.6 %all-to-all-start.2 = ((bf16[16,2,64,512]{3,2,1,0:T(8,128)(2,1)}), bf16[16,2,64,512]{3,2,1,0:T(8,128)(2,1)S(1)}, u32[]{:S(2)}, u32[]{:S(2)}) async-start(bf16[16,2,64,512]{3,2,1,0:T(8,128)(2,1)} %get-tuple-element.62), calls=%async_computation.2 | async-start | bytes 4194304 | tf_op jit(solution)/shard_map/cond/branch_1_fun/all_to_all | solution.py:385
  211.5 12.3 %product.3.left_hbm = bf16[2,1024,1024]{2,1,0:T(8,128)(2,1)S(1)} custom-call(bf16[2,1024,1024]{2,1,0:T(8,128)(2,1)} %get-tuple-element.59.left, bf16[16,2,64,1024]{3,2,1,0:T(8,128)(2,1)} %get-tuple-element.60.right), custom_call_target="tpu_custom_call" | custom-call | tf_op jit(solution)/shard_map/cond/branch_1_fun/product/pallas_call | solution.py:258
  223.8 2.1 copy-done.1
  225.9 31.5 %all-to-all-done.2.right_hbm = bf16[16,2,64,512]{3,2,1,0:T(8,128)(2,1)S(1)} async-done(((bf16[16,2,64,512]{3,2,1,0:T(8,128)(2,1)}), bf16[16,2,64,512]{3,2,1,0:T(8,128)(2,1)S(1)}, u32[]{:S(2)}, u32[]{:S(2)}) %all-to-all-start.2) | async-done | bytes 2097184 | tf_op jit(solution)/shard_map/cond/branch_1_fun/all_to_all | solution.py:385
  257.4 6.4 %all-to-all-start.3 = ((bf16[16,2,64,512]{3,2,1,0:T(8,128)(2,1)}), bf16[16,2,64,512]{3,2,1,0:T(8,128)(2,1)}, u32[]{:S(2)}, u32[]{:S(2)}) async-start(bf16[16,2,64,512]{3,2,1,0:T(8,128)(2,1)} %get-tuple-element.72), calls=%async_computation.3 | async-start | bytes 4194304 | tf_op jit(solution)/shard_map/cond/branch_1_fun/all_to_all | solution.py:385
  263.9 8.3 %panels.6 = (bf16[4,2,64,512]{3,2,1,0:T(8,128)(2,1)}, bf16[4,2,64,512]{3,2,1,0:T(8,128)(2,1)}, bf16[4,2,64,512]{3,2,1,0:T(8,128)(2,1)}, bf16[4,2,64,512]{3,2,1,0:T(8,128)(2,1)}) custom-call(s32[1]{0:T(128)} %get-tuple-element.58.place, bf16[2,1024,1024]{2,1,0:T(8,128)(2,1)} %copy-done.1, bf16[16,2,64,512]{3,2,1,0:T(8,128)(2,1)} %copy-done.7), custom_call_target="tpu_custom_call" | custom-call | tf_op jit(solution)/shard_map/cond/branch_1_fun/panels/pallas_call | solution.py:303
  272.4 1.5 collective-permute-start.13
  274.4 20.1 %collective-permute-done.13.refs_2_ = bf16[4,2,64,512]{3,2,1,0:T(8,128)(2,1)S(1)} collective-permute-done((bf16[4,2,64,512]{3,2,1,0:T(8,128)(2,1)}, bf16[4,2,64,512]{3,2,1,0:T(8,128)(2,1)S(1)}, u32[]{:S(2)}, u32[]{:S(2)}) %collective-permute-start.13) | collective-permute-done | bytes 524320 | tf_op jit(solution)/shard_map/cond/branch_1_fun/ppermute | solution.py:393
  294.5 17.1 %collective-permute-done.14.refs_3_ = bf16[4,2,64,512]{3,2,1,0:T(8,128)(2,1)S(1)} collective-permute-done((bf16[4,2,64,512]{3,2,1,0:T(8,128)(2,1)}, bf16[4,2,64,512]{3,2,1,0:T(8,128)(2,1)S(1)}, u32[]{:S(2)}, u32[]{:S(2)}) %collective-permute-start.14) | collective-permute-done | bytes 524320 | tf_op jit(solution)/shard_map/cond/branch_1_fun/ppermute | solution.py:393
  312.6 1.4 partial_sums.6
  314.0 8.3 %panels.7 = (bf16[4,2,64,512]{3,2,1,0:T(8,128)(2,1)}, bf16[4,2,64,512]{3,2,1,0:T(8,128)(2,1)}, bf16[4,2,64,512]{3,2,1,0:T(8,128)(2,1)}, bf16[4,2,64,512]{3,2,1,0:T(8,128)(2,1)}) custom-call(s32[1]{0:T(128)} %get-tuple-element.58.place, bf16[2,1024,1024]{2,1,0:T(8,128)(2,1)} %copy-done.1, bf16[16,2,64,512]{3,2,1,0:T(8,128)(2,1)} %all-to-all-done.3.right_hbm), custom_call_target="tpu_custom_call" | custom-call | tf_op jit(solution)/shard_map/cond/branch_1_fun/panels/pallas_call | solution.py:303
  322.8 1.5 collective-permute-start.19
  324.8 2.6 collective-permute-start.16
  327.8 10.0 %collective-permute-done.19.refs_2_ = bf16[4,2,64,512]{3,2,1,0:T(8,128)(2,1)S(1)} collective-permute-done((bf16[4,2,64,512]{3,2,1,0:T(8,128)(2,1)}, bf16[4,2,64,512]{3,2,1,0:T(8,128)(2,1)S(1)}, u32[]{:S(2)}, u32[]{:S(2)}) %collective-permute-start.19) | collective-permute-done | bytes 524320 | tf_op jit(solution)/shard_map/cond/branch_1_fun/ppermute | solution.py:393
  337.7 9.7 %collective-permute-done.20.refs_3_ = bf16[4,2,64,512]{3,2,1,0:T(8,128)(2,1)S(1)} collective-permute-done((bf16[4,2,64,512]{3,2,1,0:T(8,128)(2,1)}, bf16[4,2,64,512]{3,2,1,0:T(8,128)(2,1)S(1)}, u32[]{:S(2)}, u32[]{:S(2)}) %collective-permute-start.20) | collective-permute-done | bytes 524320 | tf_op jit(solution)/shard_map/cond/branch_1_fun/ppermute | solution.py:393
  348.5 1.4 partial_sums.7
  350.9 2.4 collective-permute-start.22
  353.8 26.1 %collective-permute-done.17.refs_3_ = bf16[3,2,64,512]{3,2,1,0:T(8,128)(2,1)S(1)} collective-permute-done((bf16[3,2,64,512]{3,2,1,0:T(8,128)(2,1)S(1)}, bf16[3,2,64,512]{3,2,1,0:T(8,128)(2,1)S(1)}, u32[]{:S(2)}, u32[]{:S(2)}) %collective-permute-start.17) | collective-permute-done | bytes 393248 | tf_op jit(solution)/shard_map/cond/branch_1_fun/ppermute | solution.py:393
  379.8 7.6 %collective-permute-done.22.refs_6_ = bf16[3,2,64,512]{3,2,1,0:T(8,128)(2,1)S(1)} collective-permute-done((bf16[3,2,64,512]{3,2,1,0:T(8,128)(2,1)S(1)}, bf16[3,2,64,512]{3,2,1,0:T(8,128)(2,1)S(1)}, u32[]{:S(2)}, u32[]{:S(2)}) %collective-permute-start.22) | collective-permute-done | bytes 393248 | tf_op jit(solution)/shard_map/cond/branch_1_fun/ppermute | solution.py:393
  387.5 8.7 %collective-permute-done.23.refs_7_ = bf16[3,2,64,512]{3,2,1,0:T(8,128)(2,1)S(1)} collective-permute-done((bf16[3,2,64,512]{3,2,1,0:T(8,128)(2,1)S(1)}, bf16[3,2,64,512]{3,2,1,0:T(8,128)(2,1)S(1)}, u32[]{:S(2)}, u32[]{:S(2)}) %collective-permute-start.23) | collective-permute-done | bytes 393248 | tf_op jit(solution)/shard_map/cond/branch_1_fun/ppermute | solution.py:393
  396.1 1.9 diagrams.3
  (27 shorter events, 9.0 us)
Async XLA Ops:
  10.5 97.1 %all-to-all-start.4 = ((bf16[16,2,64,1024]{3,2,1,0:T(8,128)(2,1)}), bf16[16,2,64,1024]{3,2,1,0:T(8,128)(2,1)}, u32[]{:S(2)}, u32[]{:S(2)}) async-start(bf16[16,2,64,1024]{3,2,1,0:T(8,128)(2,1)} %pick.4), calls=%async_computation.4 | async-start | bytes 8388608 | tf_op jit(solution)/shard_map/all_to_all | solution.py:385
  107.6 97.4 %all-to-all-start.5 = ((bf16[16,2,64,1024]{3,2,1,0:T(8,128)(2,1)}), bf16[16,2,64,1024]{3,2,1,0:T(8,128)(2,1)}, u32[]{:S(2)}, u32[]{:S(2)}) async-start(bf16[16,2,64,1024]{3,2,1,0:T(8,128)(2,1)} %pick.5), calls=%async_computation.5 | async-start | bytes 8388608 | tf_op jit(solution)/shard_map/all_to_all | solution.py:385
  114.2 7.9 %collective-permute-start.24 = (bf16[16,2,64,1024]{3,2,1,0:T(8,128)(2,1)}, bf16[16,2,64,1024]{3,2,1,0:T(8,128)(2,1)}, u32[]{:S(2)}, u32[]{:S(2)}) collective-permute-start(bf16[16,2,64,1024]{3,2,1,0:T(8,128)(2,1)} %all-to-all-done.4.own), channel_id=1, source_target_pairs={{0,1},{1,0},{2,3},{3,2},{4,5},{5,4},{6,7},{7,6},{8,9},{9,8},{10,11... | collective-permute-start | bytes 12582920 | tf_op jit(solution)/shard_map/ppermute | solution.py:393
  205.0 52.4 %all-to-all-start.2 = ((bf16[16,2,64,512]{3,2,1,0:T(8,128)(2,1)}), bf16[16,2,64,512]{3,2,1,0:T(8,128)(2,1)S(1)}, u32[]{:S(2)}, u32[]{:S(2)}) async-start(bf16[16,2,64,512]{3,2,1,0:T(8,128)(2,1)} %get-tuple-element.62), calls=%async_computation.2 | async-start | bytes 4194304 | tf_op jit(solution)/shard_map/cond/branch_1_fun/all_to_all | solution.py:385
  223.8 2.1 copy-start.1
  257.4 6.5 %copy-start.7 = (bf16[16,2,64,512]{3,2,1,0:T(8,128)(2,1)}, bf16[16,2,64,512]{3,2,1,0:T(8,128)(2,1)S(1)}, u32[]{:S(2)}) copy-start(bf16[16,2,64,512]{3,2,1,0:T(8,128)(2,1)S(1)} %all-to-all-done.2.right_hbm) | copy-start | bytes 6291460 | tf_op jit(solution)/shard_map/cond
  257.4 56.6 %all-to-all-start.3 = ((bf16[16,2,64,512]{3,2,1,0:T(8,128)(2,1)}), bf16[16,2,64,512]{3,2,1,0:T(8,128)(2,1)}, u32[]{:S(2)}, u32[]{:S(2)}) async-start(bf16[16,2,64,512]{3,2,1,0:T(8,128)(2,1)} %get-tuple-element.72), calls=%async_computation.3 | async-start | bytes 4194304 | tf_op jit(solution)/shard_map/cond/branch_1_fun/all_to_all | solution.py:385
  272.2 2.2 collective-permute-start.12
  272.4 22.1 %collective-permute-start.13 = (bf16[4,2,64,512]{3,2,1,0:T(8,128)(2,1)}, bf16[4,2,64,512]{3,2,1,0:T(8,128)(2,1)S(1)}, u32[]{:S(2)}, u32[]{:S(2)}) collective-permute-start(bf16[4,2,64,512]{3,2,1,0:T(8,128)(2,1)} %get-tuple-element.65), channel_id=1, source_target_pairs={{0,2},{1,3},{2,0},{3,1},{4,6},{5,7},{6,4},{7,5},{8,10},{9,11},{10,... | collective-permute-start | bytes 1572872 | tf_op jit(solution)/shard_map/cond/branch_1_fun/ppermute | solution.py:393
  273.9 37.7 %collective-permute-start.14 = (bf16[4,2,64,512]{3,2,1,0:T(8,128)(2,1)}, bf16[4,2,64,512]{3,2,1,0:T(8,128)(2,1)S(1)}, u32[]{:S(2)}, u32[]{:S(2)}) collective-permute-start(bf16[4,2,64,512]{3,2,1,0:T(8,128)(2,1)} %get-tuple-element.66), channel_id=1, source_target_pairs={{0,3},{1,2},{2,1},{3,0},{4,7},{5,6},{6,5},{7,4},{8,11},{9,10},{10,... | collective-permute-start | bytes 1572872 | tf_op jit(solution)/shard_map/cond/branch_1_fun/ppermute | solution.py:393
  311.5 1.0 copy-start.5
  322.3 5.1 %collective-permute-start.18 = (bf16[4,2,64,512]{3,2,1,0:T(8,128)(2,1)}, bf16[4,2,64,512]{3,2,1,0:T(8,128)(2,1)S(1)}, u32[]{:S(2)}, u32[]{:S(2)}) collective-permute-start(bf16[4,2,64,512]{3,2,1,0:T(8,128)(2,1)} %get-tuple-element.75), channel_id=1, source_target_pairs={{0,1},{1,0},{2,3},{3,2},{4,5},{5,4},{6,7},{7,6},{8,9},{9,8},{10,11... | collective-permute-start | bytes 1572872 | tf_op jit(solution)/shard_map/cond/branch_1_fun/ppermute | solution.py:393
  322.8 15.0 %collective-permute-start.19 = (bf16[4,2,64,512]{3,2,1,0:T(8,128)(2,1)}, bf16[4,2,64,512]{3,2,1,0:T(8,128)(2,1)S(1)}, u32[]{:S(2)}, u32[]{:S(2)}) collective-permute-start(bf16[4,2,64,512]{3,2,1,0:T(8,128)(2,1)} %get-tuple-element.76), channel_id=1, source_target_pairs={{0,2},{1,3},{2,0},{3,1},{4,6},{5,7},{6,4},{7,5},{8,10},{9,11},{10,... | collective-permute-start | bytes 1572872 | tf_op jit(solution)/shard_map/cond/branch_1_fun/ppermute | solution.py:393
  324.2 23.2 %collective-permute-start.20 = (bf16[4,2,64,512]{3,2,1,0:T(8,128)(2,1)}, bf16[4,2,64,512]{3,2,1,0:T(8,128)(2,1)S(1)}, u32[]{:S(2)}, u32[]{:S(2)}) collective-permute-start(bf16[4,2,64,512]{3,2,1,0:T(8,128)(2,1)} %get-tuple-element.77), channel_id=1, source_target_pairs={{0,3},{1,2},{2,1},{3,0},{4,7},{5,6},{6,5},{7,4},{8,11},{9,10},{10,... | collective-permute-start | bytes 1572872 | tf_op jit(solution)/shard_map/cond/branch_1_fun/ppermute | solution.py:393
  324.2 29.1 %collective-permute-start.15 = (bf16[3,2,64,512]{3,2,1,0:T(8,128)(2,1)S(1)}, bf16[3,2,64,512]{3,2,1,0:T(8,128)(2,1)S(1)}, u32[]{:S(2)}, u32[]{:S(2)}) collective-permute-start(bf16[3,2,64,512]{3,2,1,0:T(8,128)(2,1)S(1)} %get-tuple-element.68), channel_id=1, source_target_pairs={{0,4},{1,5},{2,6},{3,7},{4,0},{5,1},{6,2},{7,3},{8,12},{9,13},{10,... | collective-permute-start | bytes 1179656 | tf_op jit(solution)/shard_map/cond/branch_1_fun/ppermute | solution.py:393
  324.8 29.0 %collective-permute-start.16 = (bf16[3,2,64,512]{3,2,1,0:T(8,128)(2,1)S(1)}, bf16[3,2,64,512]{3,2,1,0:T(8,128)(2,1)S(1)}, u32[]{:S(2)}, u32[]{:S(2)}) collective-permute-start(bf16[3,2,64,512]{3,2,1,0:T(8,128)(2,1)S(1)} %get-tuple-element.69), channel_id=1, source_target_pairs={{0,8},{1,9},{2,10},{3,11},{4,12},{5,13},{6,14},{7,15},{8,0},{9,1},... | collective-permute-start | bytes 1179656 | tf_op jit(solution)/shard_map/cond/branch_1_fun/ppermute | solution.py:393
  327.4 52.4 %collective-permute-start.17 = (bf16[3,2,64,512]{3,2,1,0:T(8,128)(2,1)S(1)}, bf16[3,2,64,512]{3,2,1,0:T(8,128)(2,1)S(1)}, u32[]{:S(2)}, u32[]{:S(2)}) collective-permute-start(bf16[3,2,64,512]{3,2,1,0:T(8,128)(2,1)S(1)} %get-tuple-element.70), channel_id=1, source_target_pairs={{0,12},{1,13},{2,14},{3,15},{4,8},{5,9},{6,10},{7,11},{8,4},{9,5},... | collective-permute-start | bytes 1179656 | tf_op jit(solution)/shard_map/cond/branch_1_fun/ppermute | solution.py:393
  347.5 1.0 copy-start.3
  349.9 29.9 %collective-permute-start.21 = (bf16[3,2,64,512]{3,2,1,0:T(8,128)(2,1)S(1)}, bf16[3,2,64,512]{3,2,1,0:T(8,128)(2,1)S(1)}, u32[]{:S(2)}, u32[]{:S(2)}) collective-permute-start(bf16[3,2,64,512]{3,2,1,0:T(8,128)(2,1)S(1)} %get-tuple-element.79), channel_id=1, source_target_pairs={{0,4},{1,5},{2,6},{3,7},{4,0},{5,1},{6,2},{7,3},{8,12},{9,13},{10,... | collective-permute-start | bytes 1179656 | tf_op jit(solution)/shard_map/cond/branch_1_fun/ppermute | solution.py:393
  350.9 36.5 %collective-permute-start.22 = (bf16[3,2,64,512]{3,2,1,0:T(8,128)(2,1)S(1)}, bf16[3,2,64,512]{3,2,1,0:T(8,128)(2,1)S(1)}, u32[]{:S(2)}, u32[]{:S(2)}) collective-permute-start(bf16[3,2,64,512]{3,2,1,0:T(8,128)(2,1)S(1)} %get-tuple-element.80), channel_id=1, source_target_pairs={{0,8},{1,9},{2,10},{3,11},{4,12},{5,13},{6,14},{7,15},{8,0},{9,1},... | collective-permute-start | bytes 1179656 | tf_op jit(solution)/shard_map/cond/branch_1_fun/ppermute | solution.py:393
  353.3 42.8 %collective-permute-start.23 = (bf16[3,2,64,512]{3,2,1,0:T(8,128)(2,1)S(1)}, bf16[3,2,64,512]{3,2,1,0:T(8,128)(2,1)S(1)}, u32[]{:S(2)}, u32[]{:S(2)}) collective-permute-start(bf16[3,2,64,512]{3,2,1,0:T(8,128)(2,1)S(1)} %get-tuple-element.81), channel_id=1, source_target_pairs={{0,12},{1,13},{2,14},{3,15},{4,8},{5,9},{6,10},{7,11},{8,4},{9,5},... | collective-permute-start | bytes 1179656 | tf_op jit(solution)/shard_map/cond/branch_1_fun/ppermute | solution.py:393
  398.4 1.3 copy-start.8
where the time goes:
time: 401 us; the launch traced here: 400 us
  waiting for transfers between devices  283 us (71%)
  Pallas kernels  71.2 us (18%)
  starting transfers between devices  36.9 us (9%)
  local copies, waits for them, and re-layouts  7.35 us (2%)
    all_to_all x4, waiting for transfers between devices, exchange(): return lax.all_to_all(x, 'node', split_axis=0, concat_axis=0, tiled=True)  183 us
    ppermute x13, waiting for transfers between devices, swap(): return lax.ppermute(x, 'node', [(i, i ^ shift) for i in range(size)])  99.7 us
    all_to_all x4, starting transfers between devices, exchange(): return lax.all_to_all(x, 'node', split_axis=0, concat_axis=0, tiled=True)  25.9 us
    pallas_call x1, Pallas kernels, left_pair(): pl.pallas_call(left_kernel, out_shape=jax.ShapeDtypeStruct((2, order, ord...  16.9 us
    pallas_call x2, Pallas kernels, panels_of(): pl.pallas_call(panels_kernel, out_shape=[jax.ShapeDtypeStruct((count // S...  16.6 us
    pallas_call x4, Pallas kernels, pick(): pl.pallas_call(functools.partial(pick_kernel, row, start), out_shape=jax....  16.1 us
    pallas_call x1, Pallas kernels, product(): pl.pallas_call(product_kernel, out_shape=jax.ShapeDtypeStruct(left.shape,...  12.3 us
    ppermute x13, starting transfers between devices, swap(): return lax.ppermute(x, 'node', [(i, i ^ shift) for i in range(size)])  11.1 us
  transfers between devices with their start and end apart: 17, of which 12 were waited for; matrix products, arithmetic and copies ran while one was open for 0% of the time, Pallas kernels for 13%

commit v1 on v0

--- a/solution.py
+++ b/solution.py
@@ -92,7 +92,7 @@
         table[3, device] = prod_flag[k]
         d = diag[s]
         owner = device // SET
-        code = SET * jnp.bitwise_xor(owner, mine)
+        code = SET * owner
         earlier = table[4, d]
         shared = jnp.logical_and(earlier >= 0, earlier // SET == code // SET)
         slot = jnp.where(shared, earlier - code, slots[owner])
@@ -177,6 +177,88 @@
     )(table, nodes)
 
 
+def pick_sets_kernel(row, place, table, nodes, *refs):
+    outs, (held, reads, writes) = refs[:SET], refs[SET:]
+    sets = outs[0].shape[0]
+    own = lax.rem(place[0], SET)
+    which = [(s, q) for s in range(SET) for q in range(sets)]
+
+    def read(s, q):
+        node = nodes.at[table[row, SET * q + jnp.bitwise_xor(own, s)]]
+        return pltpu.make_async_copy(node, held.at[s, q], reads.at[s, q])
+
+    def write(s, q):
+        return pltpu.make_async_copy(held.at[s, q], outs[s].at[q], writes.at[s, q])
+
+    for s, q in which:
+        read(s, q).start()
+    for s, q in which:
+        read(s, q).wait()
+        write(s, q).start()
+    for s, q in which:
+        write(s, q).wait()
+
+
+def pick_sets(table, place, nodes, row):
+    sets = table.shape[1] // SET
+    shape = nodes.shape[1:]
+    return pl.pallas_call(
+        functools.partial(pick_sets_kernel, row),
+        out_shape=[jax.ShapeDtypeStruct((sets,) + shape, nodes.dtype)] * SET,
+        in_specs=[SMEM, SMEM, HBM],
+        out_specs=[HBM] * SET,
+        scratch_shapes=[
+            pltpu.VMEM((SET, sets) + shape, nodes.dtype),
+            pltpu.SemaphoreType.DMA((SET, sets)),
+            pltpu.SemaphoreType.DMA((SET, sets)),
+        ],
+        compiler_params=params(WHOLE_VMEM_BYTES),
+        name="pick_sets",
+    )(place, table, nodes)
+
+
+def regroup_kernel(starts, *refs):
+    pieces, outs, (held, reads, writes) = refs[:SET], refs[SET:-3], refs[-3:]
+    sets = pieces[0].shape[0]
+    which = [(s, q) for q in range(sets) for s in range(SET)]
+
+    def read(s, q):
+        return pltpu.make_async_copy(pieces[s].at[q], held.at[s, q], reads.at[s, q])
+
+    def write(s, q, j):
+        columns = held.at[s, q, :, :, pl.ds(starts[j], outs[j].shape[4])]
+        return pltpu.make_async_copy(columns, outs[j].at[q, s], writes.at[s, q, j])
+
+    for s, q in which:
+        read(s, q).start()
+    for s, q in which:
+        read(s, q).wait()
+        for j in range(len(starts)):
+            write(s, q, j).start()
+    for s, q in which:
+        for j in range(len(starts)):
+            write(s, q, j).wait()
+
+
+def regroup(pieces, widths):
+    sets, two, rows, _ = pieces[0].shape
+    dtype = pieces[0].dtype
+    starts = [sum(widths[:j]) for j in range(len(widths))]
+    return pl.pallas_call(
+        functools.partial(regroup_kernel, starts),
+        out_shape=[jax.ShapeDtypeStruct((sets, SET, two, rows, w), dtype) for w in widths],
+        in_specs=[HBM] * SET,
+        out_specs=[HBM] * len(widths),
+        scratch_shapes=[
+            pltpu.VMEM((SET,) + pieces[0].shape, dtype),
+            pltpu.SemaphoreType.DMA((SET, sets)),
+            pltpu.SemaphoreType.DMA((SET, sets, len(widths))),
+        ],
+        compiler_params=params(WHOLE_VMEM_BYTES),
+        name="regroup",
+    )(*pieces)
+
+
 def dot(a, b):
     return jnp.dot(a, b, preferred_element_type=jnp.float32)
 
@@ -266,24 +348,30 @@
 
 
 def panels_kernel(place, left_hbm, right_hbm, *refs):
-    outs, (left, right, scratch, sems) = refs[:-4], refs[-4:]
+    outs, (left, right, scratch, sems, right_sems) = refs[:-5], refs[-5:]
     order = left.shape[2]
     width = right.shape[3]
     rows_each = right.shape[2]
     step = order // BLOCKS
     per = step // rows_each
     own = lax.rem(place[0], SET)
-    copies = [pltpu.make_async_copy(right_hbm, right, sems.at[BLOCKS])]
+    rights, lefts = [], []
+    for q in range(right_hbm.shape[0]):
+        for s in range(SET):
+            device = SET * q + jnp.bitwise_xor(own, s)
+            sem = right_sems.at[q, s]
+            rights.append(pltpu.make_async_copy(right_hbm.at[q, s], right.at[device], sem))
     for block in range(BLOCKS):
         rows = slice(block * step, (block + 1) * step)
-        copies.append(pltpu.make_async_copy(left_hbm.at[:, rows], left.at[:, rows], sems.at[block]))
-    for copy in copies:
+        lefts.append(pltpu.make_async_copy(left_hbm.at[:, rows], left.at[:, rows], sems.at[block]))
+    for copy in rights + lefts:
         copy.start()
-    copies[0].wait()
+    for copy in rights:
+        copy.wait()
     b_re = right[:, 0].reshape(order, width)
     b_im = right[:, 1].reshape(order, width)
     for block in range(BLOCKS):
-        copies[block + 1].wait()
+        lefts[block].wait()
         rows = slice(block * step, (block + 1) * step)
         a_re = left[0, rows, :]
         a_im = left[1, rows, :]
@@ -299,90 +387,127 @@
 
 
 def panels_of(place, left, right):
-    count, two, rows, width = right.shape
+    sets, _, two, rows, width = right.shape
+    whole = pltpu.VMEM((sets * SET, two, rows, width), right.dtype)
     return pl.pallas_call(
         panels_kernel,
-        out_shape=[jax.ShapeDtypeStruct((count // SET, two, rows, width), left.dtype)] * SET,
+        out_shape=[jax.ShapeDtypeStruct((sets, two, rows, width), left.dtype)] * SET,
         in_specs=[SMEM, HBM, HBM],
         out_specs=[VMEM] * SET,
         scratch_shapes=[
             pltpu.VMEM(left.shape, left.dtype),
-            pltpu.VMEM(right.shape, right.dtype),
-            pltpu.VMEM(right.shape, right.dtype),
-            pltpu.SemaphoreType.DMA((BLOCKS + 1,)),
+            whole,
+            whole,
+            pltpu.SemaphoreType.DMA((BLOCKS,)),
+            pltpu.SemaphoreType.DMA((sets, SET)),
         ],
         compiler_params=params(PANELS_VMEM_BYTES),
         name="panels",
     )(place, left, right)
 
 
-def partial_kernel(table, place, *refs):
-    pieces, outs, scratch = refs[:SET], refs[SET:-1], refs[-1]
+def sums_kernel(whole, table, place, *refs):
+    pieces, outs, rest, scratch = refs[:SET], refs[SET:-2], refs[-2], refs[-1]
     own = lax.rem(place[0], SET)
     mine = place[0] // SET
     for s, piece in enumerate(pieces):
         scratch[s] = piece[...]
-    for slot in range(outs[0].shape[0]):
+
+    def sum_at(slot, owner):
         one = jnp.bitwise_xor(table[6, slot], own)
         second = table[7, slot]
         two = jnp.bitwise_xor(jnp.maximum(second, 0), own)
-        for e, out in enumerate(outs):
-            owner = jnp.bitwise_xor(mine, e)
-            other = scratch[two, owner].astype(jnp.float32)
-            total = scratch[one, owner].astype(jnp.float32) + jnp.where(second >= 0, other, 0.0)
-            out[slot] = total.astype(out.dtype)
-
-
-def partial_sums(slots, table, place, pieces):
+        other = scratch[two, owner].astype(jnp.float32)
+        total = scratch[one, owner].astype(jnp.float32) + jnp.where(second >= 0, other, 0.0)
+        return total.astype(rest.dtype)
+
+    for slot in range(SET - 1):
+        for e in range(rest.shape[0]):
+            if whole:
+                outs[0][e, slot] = sum_at(slot, e)
+            else:
+                outs[e][slot] = sum_at(slot, jnp.bitwise_xor(mine, e))
+
+    @pl.when(table[8, 0] == SET)
+    def _():
+        for e in range(rest.shape[0]):
+            rest[e, 0] = sum_at(SET - 1, e)
+
+
+def sums_of(table, place, pieces, whole):
     sets = pieces[0].shape[0]
     shape = pieces[0].shape[1:]
-    return pl.pallas_call(
-        partial_kernel,
-        out_shape=[jax.ShapeDtypeStruct((slots,) + shape, pieces[0].dtype)] * sets,
+    dtype = pieces[0].dtype
+    outs = [jax.ShapeDtypeStruct((sets, SET - 1) + shape, dtype)]
+    if not whole:
+        outs = [jax.ShapeDtypeStruct((SET - 1,) + shape, dtype)] * sets
+    outs.append(jax.ShapeDtypeStruct((sets, 1) + shape, dtype))
+    *sums, rest = pl.pallas_call(
+        functools.partial(sums_kernel, whole),
+        out_shape=outs,
         in_specs=[SMEM, SMEM] + [VMEM] * SET,
-        out_specs=[VMEM] * sets,
-        scratch_shapes=[pltpu.VMEM((SET,) + pieces[0].shape, pieces[0].dtype)],
+        out_specs=[VMEM] * len(outs),
+        scratch_shapes=[pltpu.VMEM((SET,) + pieces[0].shape, dtype)],
         compiler_params=params(),
-        name="partial_sums",
+        name="sums",
     )(table, place, *pieces)
-
-
-def diagrams_kernel(parts, sets, table, *refs):
-    ins, out, held = refs[: parts * sets], refs[parts * sets], refs[parts * sets + 1]
-
-    start = 0
-    for j in range(parts):
-        width = ins[j * sets].shape[3]
-        for e in range(sets):
-            held[e, :, :, :, start : start + width] = ins[j * sets + e][...]
-        start += width
-
-    for d in range(out.shape[0]):
-        one, two = table[4, d], jnp.maximum(table[5, d], 0)
-        first = held[one // SET, lax.rem(one, SET)].astype(jnp.float32)
-        second = held[two // SET, lax.rem(two, SET)].astype(jnp.float32)
-        out[d] = (first + jnp.where(table[5, d] >= 0, second, 0.0)).astype(out.dtype)
-
-
-def diagrams_of(table, parts):
-    slots, two, rows, _ = parts[0][0].shape
-    sets = len(parts[0])
-    diags = table.shape[1] // 2
-    whole = sum(pieces[0].shape[3] for pieces in parts)
-    dtype = parts[0][0].dtype
-    return pl.pallas_call(
-        functools.partial(diagrams_kernel, len(parts), sets),
-        out_shape=jax.ShapeDtypeStruct((diags, two, rows, whole), dtype),
-        in_specs=[SMEM] + [VMEM] * (sets * len(parts)),
+    return sums, rest
+
+
+def diagrams_kernel(whole_parts, table, place, *refs):
+    wholes, rests = refs[:whole_parts], refs[whole_parts : 2 * whole_parts + 1]
+    pieces, (out, held) = refs[2 * whole_parts + 1 : -2], refs[-2:]
+    mine = place[0] // SET
+    for e, piece in enumerate(pieces):
+        held[jnp.bitwise_xor(mine, e)] = piece[...]
+
+    def write(wide):
+        start = 0
+        for part, rest in zip([*wholes, held], rests):
+            width = part.shape[4]
+
+            def sum_at(code):
+                owner, slot = code // SET, lax.rem(code, SET)
+                if not wide:
+                    return part[owner, slot].astype(jnp.float32)
+                usual = part[owner, jnp.minimum(slot, SET - 2)].astype(jnp.float32)
+                return jnp.where(slot == SET - 1, rest[owner, 0].astype(jnp.float32), usual)
+
+            for d in range(out.shape[0]):
+                second = sum_at(jnp.maximum(table[5, d], 0))
+                total = sum_at(table[4, d]) + jnp.where(table[5, d] >= 0, second, 0.0)
+                out[d, :, :, start : start + width] = total.astype(out.dtype)
+            start += width
+
+    @pl.when(table[8, 0] < SET)
+    def _():
+        write(False)
+
+    @pl.when(table[8, 0] == SET)
+    def _():
+        write(True)
+
+
+def diagrams_of(table, place, wholes, rests, pieces):
+    slots, two, rows, width = pieces[0].shape
+    order = width + sum(part.shape[4] for part in wholes)
+    dtype = pieces[0].dtype
+    operands = [*wholes, *rests, *pieces]
+    return pl.pallas_call(
+        functools.partial(diagrams_kernel, len(wholes)),
+        out_shape=jax.ShapeDtypeStruct((table.shape[1] // 2, two, rows, order), dtype),
+        in_specs=[SMEM, SMEM] + [VMEM] * len(operands),
         out_specs=VMEM,
-        scratch_shapes=[pltpu.VMEM((sets, slots, two, rows, whole), dtype)],
+        scratch_shapes=[pltpu.VMEM((len(pieces),) + pieces[0].shape, dtype)],
         compiler_params=params(),
         name="diagrams",
-    )(table, *[x for pieces in parts for x in pieces])
-
-
-def exchange(x):
-    return lax.all_to_all(x, "node", split_axis=0, concat_axis=0, tiled=True)
+    )(table, place, *operands)
+
+
+def exchange(x, groups=None):
+    return lax.all_to_all(
+        x, "node", split_axis=0, concat_axis=0, axis_index_groups=groups, tiled=True
+    )
 
 
 def after(x, earlier):
@@ -393,35 +518,43 @@
     return lax.ppermute(x, "node", [(i, i ^ shift) for i in range(size)])
 
 
-def tail(slots, size, table, place, picks, left, middle):
-    left_middle = product(left, middle)
-    done = middle
-    parts = []
-    for picked in picks:
-        last = exchange(after(picked, done))
-        if parts:
-            last = after(last, parts[-1][0])
-        sent = panels_of(place, left_middle, last)
-        pieces = [sent[0]] + [swap(sent[s], size, s) for s in range(1, SET)]
-        sums = partial_sums(slots, table, place, pieces)
-        done = (last, left_middle)
-        parts.append([sums[0]] + [swap(x, size, SET * e) for e, x in enumerate(sums) if e])
-    return diagrams_of(table, parts)
+def within(pieces, size):
+    return [pieces[0]] + [swap(pieces[s], size, s) for s in range(1, SET)]
 
 
 def local(size, nodes, pair_nodes, prod_left, prod_right, prod_flag, prod_diag):
     place = lax.axis_index("node").astype(jnp.int32).reshape(1)
     order = nodes.shape[3]
+    widths = [order * share // sum(SHARES) for share in SHARES]
+    across = [list(range(i, size, SET)) for i in range(SET)]
     table = route(place, pair_nodes, prod_left, prod_right, prod_flag, prod_diag)
     own = exchange(pick(table, nodes, 0, 0, order))
+    pieces = within(pick_sets(table, place, nodes, 2), size)
     other = swap(own, size, 1)
-    middle = exchange(after(pick(table, nodes, 1, 0, order), own))
+    middle = exchange(after(pick(table, nodes, 1, 0, order), (own, pieces[2])))
     left = left_pair(table, place, own, other)
-    widths = [order * share // sum(SHARES) for share in SHARES]
-    picks = [pick(table, nodes, 2, sum(widths[:j]), width) for j, width in enumerate(widths)]
-    few = functools.partial(tail, SET - 1, size)
-    many = functools.partial(tail, SET, size)
-    return lax.cond(table[8, 0] < SET, few, many, table, place, picks, left, middle)
+    sents = regroup(pieces, widths)
+    left_middle = product(left, middle)
+    done, wholes, rests = (middle, left), [], []
+    for j, sent in enumerate(sents):
+        last = exchange(after(sent, done), across)
+        done = (last, left_middle)
+        if wholes:
+            last = after(last, sums)
+        panels = within(panels_of(place, left_middle, last), size)
+        if wholes:
+            panels = after(panels, wholes[-1])
+        sums, rest = sums_of(table, place, panels, j < len(sents) - 1)
+        rests.append(rest)
+        if j < len(sents) - 1:
+            wholes.append(exchange(sums[0], across))
+    sums = [x if e == 0 else swap(x, size, SET * e) for e, x in enumerate(sums)]
+
+    def move(rests):
+        return [exchange(rest, across) for rest in rests]
+
+    rests = lax.cond(table[8, 0] < SET, lambda rests: rests, move, rests)
+    return diagrams_of(table, place, wholes, rests, sums)
 
 
 def solution(mesh):

time: 401 us -> 398 us (level)
  waiting for transfers between devices: 283 us -> 264 us
  starting transfers between devices: 36.9 us -> 43.4 us
  Pallas kernels: 71.2 us -> 76.9 us
  local copies, waits for them, and re-layouts: 7.35 us -> 11.6 us
    all_to_all x4 -> x5, waiting for transfers between devices: 183 us -> 111 us  [exchange(): lax.all_to_all(x, 'node', split_axis=0, concat_axis=0, axis_index_groups=...]
    ppermute x13, waiting for transfers between devices: 99.7 us -> 153 us  [swap(): return lax.ppermute(x, 'node', [(i, i ^ shift) for i in range(size)])]
    pallas_call x5 -> x7, Pallas kernels: 21.4 us -> 36.2 us  [the longest x2 18.6 us: panels_of(): pl.pallas_call(panels_kernel, out_shape=[jax.ShapeDtypeStruct((sets, two,...]
    unnamed x3 -> x23, local copies, waits for them, and re-layouts: 2.67 us -> 11 us
    all_to_all x4 -> x5, starting transfers between devices: 25.9 us -> 32.7 us  [exchange(): lax.all_to_all(x, 'node', split_axis=0, concat_axis=0, axis_index_groups=...]
    pallas_call x4 -> x2, Pallas kernels: 16.1 us -> 10.1 us  [pick(): pl.pallas_call(functools.partial(pick_kernel, row, start), out_shape=jax....]
    cond x8 -> x0, local copies, waits for them, and re-layouts: 4.15 us -> none
  transfers between devices with their start and end apart: 17 -> 18, of which waited for: 12 -> 15; matrix products, arithmetic and copies ran while one was open for 0% -> 0% of each run, Pallas kernels for 13% -> 15%
where the time goes in v1:
time: 398 us; the launch traced here: 397 us
  waiting for transfers between devices  264 us (66%)
  Pallas kernels  76.9 us (19%)
  starting transfers between devices  43.4 us (11%)
  local copies, waits for them, and re-layouts  11.6 us (3%)
    ppermute x13, waiting for transfers between devices, swap(): return lax.ppermute(x, 'node', [(i, i ^ shift) for i in range(size)])  153 us
    all_to_all x5, waiting for transfers between devices, exchange(): lax.all_to_all(x, 'node', split_axis=0, concat_axis=0, axis_index_groups=...  111 us
    all_to_all x5, starting transfers between devices, exchange(): lax.all_to_all(x, 'node', split_axis=0, concat_axis=0, axis_index_groups=...  32.7 us
    pallas_call x2, Pallas kernels, panels_of(): pl.pallas_call(panels_kernel, out_shape=[jax.ShapeDtypeStruct((sets, two,...  18.6 us
    pallas_call x1, Pallas kernels, left_pair(): pl.pallas_call(left_kernel, out_shape=jax.ShapeDtypeStruct((2, order, ord...  13.9 us
    pallas_call x1, Pallas kernels, product(): pl.pallas_call(product_kernel, out_shape=jax.ShapeDtypeStruct(left.shape,...  12.3 us
    unnamed x23, local copies, waits for them, and re-layouts  11 us
    ppermute x13, starting transfers between devices, swap(): return lax.ppermute(x, 'node', [(i, i ^ shift) for i in range(size)])  10.7 us
  transfers between devices with their start and end apart: 18, of which 15 were waited for; matrix products, arithmetic and copies ran while one was open for 0% of the time, Pallas kernels for 15%

profile of v1, /device:TPU:10, one launch (start us, length us, event | category | flops | bytes accessed | tf_op | source)
XLA Modules:
  0.0 397.0 jit_solution(10531727284349601783)
XLA Ops:
  1.4 4.5 %route.1.table = s32[9,16]{1,0:T(8,128)} custom-call(s32[1]{0:T(128)} %bitcast.place_ref.place, s32[16,2]{1,0:T(8,128)} %copy.7.pair_nodes, s32[16]{0:T(128)} %prod_left.1, s32[16]{0:T(128)} %prod_right.1, s32[16]{0:T(128)} %prod_flag.1, s32[16]{0:T(128)} %prod_diag.1), custom_call_target="tpu_custom_call" | custom-call | tf_op jit(solution)/shard_map/route/pallas_call | solution.py:133
  5.8 5.0 %pick.2 = bf16[16,2,64,1024]{3,2,1,0:T(8,128)(2,1)} custom-call(s32[9,16]{1,0:T(8,128)} %route.1.table, bf16[64,2,64,1024]{3,2,1,0:T(8,128)(2,1)} %nodes.5), custom_call_target="tpu_custom_call" | custom-call | tf_op jit(solution)/shard_map/pick/pallas_call | solution.py:165
  10.9 6.3 %all-to-all-start.2 = ((bf16[16,2,64,1024]{3,2,1,0:T(8,128)(2,1)}), bf16[16,2,64,1024]{3,2,1,0:T(8,128)(2,1)}, u32[]{:S(2)}, u32[]{:S(2)}) async-start(bf16[16,2,64,1024]{3,2,1,0:T(8,128)(2,1)} %pick.2), calls=%async_computation.2 | async-start | bytes 8388608 | tf_op jit(solution)/shard_map/all_to_all | solution.py:508
  17.2 4.9 %pick_sets.1 = (bf16[4,2,64,1024]{3,2,1,0:T(8,128)(2,1)}, bf16[4,2,64,1024]{3,2,1,0:T(8,128)(2,1)}, bf16[4,2,64,1024]{3,2,1,0:T(8,128)(2,1)}, bf16[4,2,64,1024]{3,2,1,0:T(8,128)(2,1)}) custom-call(s32[1]{0:T(128)} %bitcast.place_ref.place, s32[9,16]{1,0:T(8,128)} %route.1.table, bf16[64,2,64,1024]{3,2,1,0:T(8,128)(2,1)} %nodes.5), custom_call_target="tpu_custom_call" | custom-call | tf_op jit(solution)/shard_map/pick_sets/pallas_call | solution.py:205
  23.7 5.0 %pick.3 = bf16[16,2,64,1024]{3,2,1,0:T(8,128)(2,1)} custom-call(s32[9,16]{1,0:T(8,128)} %route.1.table, bf16[64,2,64,1024]{3,2,1,0:T(8,128)(2,1)} %nodes.5), custom_call_target="tpu_custom_call" | custom-call | tf_op jit(solution)/shard_map/pick/pallas_call | solution.py:165
  28.7 42.7 %collective-permute-done.1.refs_2_ = bf16[4,2,64,1024]{3,2,1,0:T(8,128)(2,1)S(1)} collective-permute-done((bf16[4,2,64,1024]{3,2,1,0:T(8,128)(2,1)}, bf16[4,2,64,1024]{3,2,1,0:T(8,128)(2,1)S(1)}, u32[]{:S(2)}, u32[]{:S(2)}) %collective-permute-start.1) | collective-permute-done | bytes 1048608 | tf_op jit(solution)/shard_map/ppermute | solution.py:518
  71.5 36.6 %all-to-all-done.2.own = bf16[16,2,64,1024]{3,2,1,0:T(8,128)(2,1)} async-done(((bf16[16,2,64,1024]{3,2,1,0:T(8,128)(2,1)}), bf16[16,2,64,1024]{3,2,1,0:T(8,128)(2,1)}, u32[]{:S(2)}, u32[]{:S(2)}) %all-to-all-start.2) | async-done | bytes 4194336 | tf_op jit(solution)/shard_map/all_to_all | solution.py:508
  108.1 6.6 %all-to-all-start.3 = ((bf16[16,2,64,1024]{3,2,1,0:T(8,128)(2,1)}), bf16[16,2,64,1024]{3,2,1,0:T(8,128)(2,1)}, u32[]{:S(2)}, u32[]{:S(2)}) async-start(bf16[16,2,64,1024]{3,2,1,0:T(8,128)(2,1)} %pick.3), calls=%async_computation.3 | async-start | bytes 8388608 | tf_op jit(solution)/shard_map/all_to_all | solution.py:508
  116.5 7.1 %collective-permute-done.2.refs_1_ = bf16[4,2,64,1024]{3,2,1,0:T(8,128)(2,1)S(1)} collective-permute-done((bf16[4,2,64,1024]{3,2,1,0:T(8,128)(2,1)}, bf16[4,2,64,1024]{3,2,1,0:T(8,128)(2,1)S(1)}, u32[]{:S(2)}, u32[]{:S(2)}) %collective-permute-start.2) | collective-permute-done | bytes 1048608 | tf_op jit(solution)/shard_map/ppermute | solution.py:518
  123.5 44.9 %collective-permute-done.3.refs_3_ = bf16[4,2,64,1024]{3,2,1,0:T(8,128)(2,1)S(1)} collective-permute-done((bf16[4,2,64,1024]{3,2,1,0:T(8,128)(2,1)S(1)}, bf16[4,2,64,1024]{3,2,1,0:T(8,128)(2,1)S(1)}, u32[]{:S(2)}, u32[]{:S(2)}) %collective-permute-start.3) | collective-permute-done | bytes 1048608 | tf_op jit(solution)/shard_map/ppermute | solution.py:518
  169.5 4.0 %regroup.1 = (bf16[4,4,2,64,512]{4,3,2,1,0:T(8,128)(2,1)}, bf16[4,4,2,64,512]{4,3,2,1,0:T(8,128)(2,1)}) custom-call(bf16[4,2,64,1024]{3,2,1,0:T(8,128)(2,1)} %get-tuple-element.48.refs_0_, bf16[4,2,64,1024]{3,2,1,0:T(8,128)(2,1)} %copy-done.8, bf16[4,2,64,1024]{3,2,1,0:T(8,128)(2,1)} %copy-done.7, bf16[4,2,64,1024]{3,2,1,0:T(8,128)(2,1)} %copy-done.9), custom_call_target="tpu_custom_call" | custom-call | tf_op jit(solution)/shard_map/regroup/pallas_call | solution.py:247
  173.5 13.9 %left_pair.1.left = bf16[2,1024,1024]{2,1,0:T(8,128)(2,1)S(1)} custom-call(s32[9,16]{1,0:T(8,128)S(1)} %copy-done.4, s32[1]{0:T(128)} %bitcast.place_ref.place, bf16[16,2,64,1024]{3,2,1,0:T(8,128)(2,1)} %all-to-all-done.2.own, bf16[16,2,64,1024]{3,2,1,0:T(8,128)(2,1)} %collective-permute-done.other), custom_call_target="tpu_custom_call" | custom-call | tf_op jit(solution)/shard_map/left_pair/pallas_call | solution.py:310
  187.3 2.0 copy-done.1
  189.3 16.2 %all-to-all-done.3.right = bf16[16,2,64,1024]{3,2,1,0:T(8,128)(2,1)} async-done(((bf16[16,2,64,1024]{3,2,1,0:T(8,128)(2,1)}), bf16[16,2,64,1024]{3,2,1,0:T(8,128)(2,1)}, u32[]{:S(2)}, u32[]{:S(2)}) %all-to-all-start.3) | async-done | bytes 4194336 | tf_op jit(solution)/shard_map/all_to_all | solution.py:508
  205.6 6.0 %all-to-all-start.4 = ((bf16[4,4,2,64,512]{4,3,2,1,0:T(8,128)(2,1)}), bf16[4,4,2,64,512]{4,3,2,1,0:T(8,128)(2,1)S(1)}, u32[]{:S(2)}, u32[]{:S(2)}) async-start(bf16[4,4,2,64,512]{4,3,2,1,0:T(8,128)(2,1)} %get-tuple-element.52), calls=%async_computation.4 | async-start | bytes 4194304 | tf_op jit(solution)/shard_map/all_to_all | solution.py:508
  211.6 12.3 %product.1.left_hbm = bf16[2,1024,1024]{2,1,0:T(8,128)(2,1)S(1)} custom-call(bf16[2,1024,1024]{2,1,0:T(8,128)(2,1)} %copy-done.1, bf16[16,2,64,1024]{3,2,1,0:T(8,128)(2,1)} %all-to-all-done.3.right), custom_call_target="tpu_custom_call" | custom-call | tf_op jit(solution)/shard_map/product/pallas_call | solution.py:340
  223.9 2.0 copy-done
  225.9 30.5 %all-to-all-done.4.right_hbm = bf16[4,4,2,64,512]{4,3,2,1,0:T(8,128)(2,1)S(1)} async-done(((bf16[4,4,2,64,512]{4,3,2,1,0:T(8,128)(2,1)}), bf16[4,4,2,64,512]{4,3,2,1,0:T(8,128)(2,1)S(1)}, u32[]{:S(2)}, u32[]{:S(2)}) %all-to-all-start.4) | async-done | bytes 2097184 | tf_op jit(solution)/shard_map/all_to_all | solution.py:508
  257.6 7.0 %all-to-all-start.6 = ((bf16[4,4,2,64,512]{4,3,2,1,0:T(8,128)(2,1)}), bf16[4,4,2,64,512]{4,3,2,1,0:T(8,128)(2,1)S(1)}, u32[]{:S(2)}, u32[]{:S(2)}) async-start(bf16[4,4,2,64,512]{4,3,2,1,0:T(8,128)(2,1)} %get-tuple-element.60), calls=%async_computation.6 | async-start | bytes 4194304 | tf_op jit(solution)/shard_map/all_to_all | solution.py:508
  264.6 9.2 %panels.2 = (bf16[4,2,64,512]{3,2,1,0:T(8,128)(2,1)}, bf16[4,2,64,512]{3,2,1,0:T(8,128)(2,1)}, bf16[4,2,64,512]{3,2,1,0:T(8,128)(2,1)}, bf16[4,2,64,512]{3,2,1,0:T(8,128)(2,1)}) custom-call(s32[1]{0:T(128)} %bitcast.place_ref.place, bf16[2,1024,1024]{2,1,0:T(8,128)(2,1)} %copy-done, bf16[4,4,2,64,512]{4,3,2,1,0:T(8,128)(2,1)} %copy-done.6), custom_call_target="tpu_custom_call" | custom-call | tf_op jit(solution)/shard_map/panels/pallas_call | solution.py:392
  276.1 12.9 %collective-permute-done.5.refs_2_ = bf16[4,2,64,512]{3,2,1,0:T(8,128)(2,1)S(1)} collective-permute-done((bf16[4,2,64,512]{3,2,1,0:T(8,128)(2,1)}, bf16[4,2,64,512]{3,2,1,0:T(8,128)(2,1)S(1)}, u32[]{:S(2)}, u32[]{:S(2)}) %collective-permute-start.5) | collective-permute-done | bytes 524320 | tf_op jit(solution)/shard_map/ppermute | solution.py:518
  288.9 10.3 %collective-permute-done.6.refs_3_ = bf16[4,2,64,512]{3,2,1,0:T(8,128)(2,1)S(1)} collective-permute-done((bf16[4,2,64,512]{3,2,1,0:T(8,128)(2,1)}, bf16[4,2,64,512]{3,2,1,0:T(8,128)(2,1)S(1)}, u32[]{:S(2)}, u32[]{:S(2)}) %collective-permute-start.6) | collective-permute-done | bytes 524320 | tf_op jit(solution)/shard_map/ppermute | solution.py:518
  300.3 2.8 sums.2
  303.1 6.1 %all-to-all-done.6.right_hbm = bf16[4,4,2,64,512]{4,3,2,1,0:T(8,128)(2,1)S(1)} async-done(((bf16[4,4,2,64,512]{4,3,2,1,0:T(8,128)(2,1)}), bf16[4,4,2,64,512]{4,3,2,1,0:T(8,128)(2,1)S(1)}, u32[]{:S(2)}, u32[]{:S(2)}) %all-to-all-start.6) | async-done | bytes 2097184 | tf_op jit(solution)/shard_map/all_to_all | solution.py:508
  310.5 6.8 %all-to-all-start.5 = ((bf16[4,3,2,64,512]{4,3,2,1,0:T(8,128)(2,1)}), bf16[4,3,2,64,512]{4,3,2,1,0:T(8,128)(2,1)S(1)}, u32[]{:S(2)}, u32[]{:S(2)}) async-start(bf16[4,3,2,64,512]{4,3,2,1,0:T(8,128)(2,1)} %get-tuple-element.57), calls=%async_computation.5 | async-start | bytes 3145728 | tf_op jit(solution)/shard_map/all_to_all | solution.py:508
  317.3 9.3 %panels.3 = (bf16[4,2,64,512]{3,2,1,0:T(8,128)(2,1)}, bf16[4,2,64,512]{3,2,1,0:T(8,128)(2,1)}, bf16[4,2,64,512]{3,2,1,0:T(8,128)(2,1)}, bf16[4,2,64,512]{3,2,1,0:T(8,128)(2,1)}) custom-call(s32[1]{0:T(128)} %bitcast.place_ref.place, bf16[2,1024,1024]{2,1,0:T(8,128)(2,1)} %copy-done, bf16[4,4,2,64,512]{4,3,2,1,0:T(8,128)(2,1)} %copy-done.5), custom_call_target="tpu_custom_call" | custom-call | tf_op jit(solution)/shard_map/panels/pallas_call | solution.py:392
  328.6 21.9 %all-to-all-done.5.refs_0_ = bf16[4,3,2,64,512]{4,3,2,1,0:T(8,128)(2,1)S(1)} async-done(((bf16[4,3,2,64,512]{4,3,2,1,0:T(8,128)(2,1)}), bf16[4,3,2,64,512]{4,3,2,1,0:T(8,128)(2,1)S(1)}, u32[]{:S(2)}, u32[]{:S(2)}) %all-to-all-start.5) | async-done | bytes 1572896 | tf_op jit(solution)/shard_map/all_to_all | solution.py:508
  353.1 2.6 sums.3
  360.4 12.9 %collective-permute-done.10.refs_4_ = bf16[3,2,64,512]{3,2,1,0:T(8,128)(2,1)S(1)} collective-permute-done((bf16[3,2,64,512]{3,2,1,0:T(8,128)(2,1)}, bf16[3,2,64,512]{3,2,1,0:T(8,128)(2,1)S(1)}, u32[]{:S(2)}, u32[]{:S(2)}) %collective-permute-start.10) | collective-permute-done | bytes 393248 | tf_op jit(solution)/shard_map/ppermute | solution.py:518
  373.2 12.1 %collective-permute-done.11.refs_5_ = bf16[3,2,64,512]{3,2,1,0:T(8,128)(2,1)S(1)} collective-permute-done((bf16[3,2,64,512]{3,2,1,0:T(8,128)(2,1)}, bf16[3,2,64,512]{3,2,1,0:T(8,128)(2,1)S(1)}, u32[]{:S(2)}, u32[]{:S(2)}) %collective-permute-start.11) | collective-permute-done | bytes 393248 | tf_op jit(solution)/shard_map/ppermute | solution.py:518
  385.3 8.4 %collective-permute-done.12.refs_6_ = bf16[3,2,64,512]{3,2,1,0:T(8,128)(2,1)S(1)} collective-permute-done((bf16[3,2,64,512]{3,2,1,0:T(8,128)(2,1)}, bf16[3,2,64,512]{3,2,1,0:T(8,128)(2,1)S(1)}, u32[]{:S(2)}, u32[]{:S(2)}) %collective-permute-start.12) | collective-permute-done | bytes 393248 | tf_op jit(solution)/shard_map/ppermute | solution.py:518
  393.7 3.3 diagrams.1
  (41 shorter events, 20.1 us)
Async XLA Ops:
  10.9 97.2 %all-to-all-start.2 = ((bf16[16,2,64,1024]{3,2,1,0:T(8,128)(2,1)}), bf16[16,2,64,1024]{3,2,1,0:T(8,128)(2,1)}, u32[]{:S(2)}, u32[]{:S(2)}) async-start(bf16[16,2,64,1024]{3,2,1,0:T(8,128)(2,1)} %pick.2), calls=%async_computation.2 | async-start | bytes 8388608 | tf_op jit(solution)/shard_map/all_to_all | solution.py:508
  22.1 49.3 %collective-permute-start.1 = (bf16[4,2,64,1024]{3,2,1,0:T(8,128)(2,1)}, bf16[4,2,64,1024]{3,2,1,0:T(8,128)(2,1)S(1)}, u32[]{:S(2)}, u32[]{:S(2)}) collective-permute-start(bf16[4,2,64,1024]{3,2,1,0:T(8,128)(2,1)} %get-tuple-element.46), channel_id=1, source_target_pairs={{0,2},{1,3},{2,0},{3,1},{4,6},{5,7},{6,4},{7,5},{8,10},{9,11},{10,... | collective-permute-start | bytes 3145736 | tf_op jit(solution)/shard_map/ppermute | solution.py:518
  28.7 86.5 %copy-start.10 = (bf16[4,2,64,1024]{3,2,1,0:T(8,128)(2,1)S(1)}, bf16[4,2,64,1024]{3,2,1,0:T(8,128)(2,1)}, u32[]{:S(2)}) copy-start(bf16[4,2,64,1024]{3,2,1,0:T(8,128)(2,1)} %get-tuple-element.50) | copy-start | bytes 3145732
  71.5 36.6 %copy-start.7 = (bf16[4,2,64,1024]{3,2,1,0:T(8,128)(2,1)}, bf16[4,2,64,1024]{3,2,1,0:T(8,128)(2,1)S(1)}, u32[]{:S(2)}) copy-start(bf16[4,2,64,1024]{3,2,1,0:T(8,128)(2,1)S(1)} %collective-permute-done.1.refs_2_) | copy-start | bytes 3145732
  108.1 97.5 %all-to-all-start.3 = ((bf16[16,2,64,1024]{3,2,1,0:T(8,128)(2,1)}), bf16[16,2,64,1024]{3,2,1,0:T(8,128)(2,1)}, u32[]{:S(2)}, u32[]{:S(2)}) async-start(bf16[16,2,64,1024]{3,2,1,0:T(8,128)(2,1)} %pick.3), calls=%async_computation.3 | async-start | bytes 8388608 | tf_op jit(solution)/shard_map/all_to_all | solution.py:508
  114.6 58.8 %copy-start.4 = (s32[9,16]{1,0:T(8,128)S(1)}, s32[9,16]{1,0:T(8,128)}, u32[]{:S(2)}) copy-start(s32[9,16]{1,0:T(8,128)} %route.1.table) | copy-start | bytes 1732
  114.7 58.8 %collective-permute-start = (bf16[16,2,64,1024]{3,2,1,0:T(8,128)(2,1)}, bf16[16,2,64,1024]{3,2,1,0:T(8,128)(2,1)}, u32[]{:S(2)}, u32[]{:S(2)}) collective-permute-start(bf16[16,2,64,1024]{3,2,1,0:T(8,128)(2,1)} %all-to-all-done.2.own), channel_id=1, source_target_pairs={{0,1},{1,0},{2,3},{3,2},{4,5},{5,4},{6,7},{7,6},{8,9},{9,8},{10,11... | collective-permute-start | bytes 12582920 | tf_op jit(solution)/shard_map/ppermute | solution.py:518
  114.9 8.6 %collective-permute-start.2 = (bf16[4,2,64,1024]{3,2,1,0:T(8,128)(2,1)}, bf16[4,2,64,1024]{3,2,1,0:T(8,128)(2,1)S(1)}, u32[]{:S(2)}, u32[]{:S(2)}) collective-permute-start(bf16[4,2,64,1024]{3,2,1,0:T(8,128)(2,1)} %get-tuple-element.49), channel_id=1, source_target_pairs={{0,1},{1,0},{2,3},{3,2},{4,5},{5,4},{6,7},{7,6},{8,9},{9,8},{10,11... | collective-permute-start | bytes 3145736 | tf_op jit(solution)/shard_map/ppermute | solution.py:518
  115.2 53.2 %collective-permute-start.3 = (bf16[4,2,64,1024]{3,2,1,0:T(8,128)(2,1)S(1)}, bf16[4,2,64,1024]{3,2,1,0:T(8,128)(2,1)S(1)}, u32[]{:S(2)}, u32[]{:S(2)}) collective-permute-start(bf16[4,2,64,1024]{3,2,1,0:T(8,128)(2,1)S(1)} %copy-done.10), channel_id=1, source_target_pairs={{0,3},{1,2},{2,1},{3,0},{4,7},{5,6},{6,5},{7,4},{8,11},{9,10},{10,... | collective-permute-start | bytes 3145736 | tf_op jit(solution)/shard_map/ppermute | solution.py:518
  123.5 44.9 %copy-start.8 = (bf16[4,2,64,1024]{3,2,1,0:T(8,128)(2,1)}, bf16[4,2,64,1024]{3,2,1,0:T(8,128)(2,1)S(1)}, u32[]{:S(2)}) copy-start(bf16[4,2,64,1024]{3,2,1,0:T(8,128)(2,1)S(1)} %collective-permute-done.2.refs_1_) | copy-start | bytes 3145732
  168.5 1.0 copy-start.9
  187.3 2.0 copy-start.1
  205.6 50.8 %all-to-all-start.4 = ((bf16[4,4,2,64,512]{4,3,2,1,0:T(8,128)(2,1)}), bf16[4,4,2,64,512]{4,3,2,1,0:T(8,128)(2,1)S(1)}, u32[]{:S(2)}, u32[]{:S(2)}) async-start(bf16[4,4,2,64,512]{4,3,2,1,0:T(8,128)(2,1)} %get-tuple-element.52), calls=%async_computation.4 | async-start | bytes 4194304 | tf_op jit(solution)/shard_map/all_to_all | solution.py:508
  223.9 2.0 copy-start
  256.3 1.3 copy-start.6
  257.6 51.5 %all-to-all-start.6 = ((bf16[4,4,2,64,512]{4,3,2,1,0:T(8,128)(2,1)}), bf16[4,4,2,64,512]{4,3,2,1,0:T(8,128)(2,1)S(1)}, u32[]{:S(2)}, u32[]{:S(2)}) async-start(bf16[4,4,2,64,512]{4,3,2,1,0:T(8,128)(2,1)} %get-tuple-element.60), calls=%async_computation.6 | async-start | bytes 4194304 | tf_op jit(solution)/shard_map/all_to_all | solution.py:508
  273.9 2.2 collective-permute-start.4
  273.9 15.0 %collective-permute-start.5 = (bf16[4,2,64,512]{3,2,1,0:T(8,128)(2,1)}, bf16[4,2,64,512]{3,2,1,0:T(8,128)(2,1)S(1)}, u32[]{:S(2)}, u32[]{:S(2)}) collective-permute-start(bf16[4,2,64,512]{3,2,1,0:T(8,128)(2,1)} %get-tuple-element.55), channel_id=1, source_target_pairs={{0,2},{1,3},{2,0},{3,1},{4,6},{5,7},{6,4},{7,5},{8,10},{9,11},{10,... | collective-permute-start | bytes 1572872 | tf_op jit(solution)/shard_map/ppermute | solution.py:518
  275.6 23.7 %collective-permute-start.6 = (bf16[4,2,64,512]{3,2,1,0:T(8,128)(2,1)}, bf16[4,2,64,512]{3,2,1,0:T(8,128)(2,1)S(1)}, u32[]{:S(2)}, u32[]{:S(2)}) collective-permute-start(bf16[4,2,64,512]{3,2,1,0:T(8,128)(2,1)} %get-tuple-element.56), channel_id=1, source_target_pairs={{0,3},{1,2},{2,1},{3,0},{4,7},{5,6},{6,5},{7,4},{8,11},{9,10},{10,... | collective-permute-start | bytes 1572872 | tf_op jit(solution)/shard_map/ppermute | solution.py:518
  299.3 1.0 copy-start.3
  309.2 1.3 copy-start.5
  310.5 40.0 %all-to-all-start.5 = ((bf16[4,3,2,64,512]{4,3,2,1,0:T(8,128)(2,1)}), bf16[4,3,2,64,512]{4,3,2,1,0:T(8,128)(2,1)S(1)}, u32[]{:S(2)}, u32[]{:S(2)}) async-start(bf16[4,3,2,64,512]{4,3,2,1,0:T(8,128)(2,1)} %get-tuple-element.57), calls=%async_computation.5 | async-start | bytes 3145728 | tf_op jit(solution)/shard_map/all_to_all | solution.py:508
  326.6 23.8 %collective-permute-start.7 = (bf16[4,2,64,512]{3,2,1,0:T(8,128)(2,1)}, bf16[4,2,64,512]{3,2,1,0:T(8,128)(2,1)S(1)}, u32[]{:S(2)}, u32[]{:S(2)}) collective-permute-start(bf16[4,2,64,512]{3,2,1,0:T(8,128)(2,1)} %get-tuple-element.63), channel_id=1, source_target_pairs={{0,1},{1,0},{2,3},{3,2},{4,5},{5,4},{6,7},{7,6},{8,9},{9,8},{10,11... | collective-permute-start | bytes 1572872 | tf_op jit(solution)/shard_map/ppermute | solution.py:518
  326.7 23.8 %collective-permute-start.8 = (bf16[4,2,64,512]{3,2,1,0:T(8,128)(2,1)}, bf16[4,2,64,512]{3,2,1,0:T(8,128)(2,1)S(1)}, u32[]{:S(2)}, u32[]{:S(2)}) collective-permute-start(bf16[4,2,64,512]{3,2,1,0:T(8,128)(2,1)} %get-tuple-element.64), channel_id=1, source_target_pairs={{0,2},{1,3},{2,0},{3,1},{4,6},{5,7},{6,4},{7,5},{8,10},{9,11},{10,... | collective-permute-start | bytes 1572872 | tf_op jit(solution)/shard_map/ppermute | solution.py:518
  328.4 23.7 %collective-permute-start.9 = (bf16[4,2,64,512]{3,2,1,0:T(8,128)(2,1)}, bf16[4,2,64,512]{3,2,1,0:T(8,128)(2,1)S(1)}, u32[]{:S(2)}, u32[]{:S(2)}) collective-permute-start(bf16[4,2,64,512]{3,2,1,0:T(8,128)(2,1)} %get-tuple-element.65), channel_id=1, source_target_pairs={{0,3},{1,2},{2,1},{3,0},{4,7},{5,6},{6,5},{7,4},{8,11},{9,10},{10,... | collective-permute-start | bytes 1572872 | tf_op jit(solution)/shard_map/ppermute | solution.py:518
  352.0 1.0 copy-start.2
  355.7 17.5 %collective-permute-start.10 = (bf16[3,2,64,512]{3,2,1,0:T(8,128)(2,1)}, bf16[3,2,64,512]{3,2,1,0:T(8,128)(2,1)S(1)}, u32[]{:S(2)}, u32[]{:S(2)}) collective-permute-start(bf16[3,2,64,512]{3,2,1,0:T(8,128)(2,1)} %get-tuple-element.74), channel_id=1, source_target_pairs={{0,4},{1,5},{2,6},{3,7},{4,0},{5,1},{6,2},{7,3},{8,12},{9,13},{10,... | collective-permute-start | bytes 1179656 | tf_op jit(solution)/shard_map/ppermute | solution.py:518
  357.4 27.9 %collective-permute-start.11 = (bf16[3,2,64,512]{3,2,1,0:T(8,128)(2,1)}, bf16[3,2,64,512]{3,2,1,0:T(8,128)(2,1)S(1)}, u32[]{:S(2)}, u32[]{:S(2)}) collective-permute-start(bf16[3,2,64,512]{3,2,1,0:T(8,128)(2,1)} %get-tuple-element.75), channel_id=1, source_target_pairs={{0,8},{1,9},{2,10},{3,11},{4,12},{5,13},{6,14},{7,15},{8,0},{9,1},... | collective-permute-start | bytes 1179656 | tf_op jit(solution)/shard_map/ppermute | solution.py:518
  358.6 35.1 %collective-permute-start.12 = (bf16[3,2,64,512]{3,2,1,0:T(8,128)(2,1)}, bf16[3,2,64,512]{3,2,1,0:T(8,128)(2,1)S(1)}, u32[]{:S(2)}, u32[]{:S(2)}) collective-permute-start(bf16[3,2,64,512]{3,2,1,0:T(8,128)(2,1)} %get-tuple-element.76), channel_id=1, source_target_pairs={{0,12},{1,13},{2,14},{3,15},{4,8},{5,9},{6,10},{7,11},{8,4},{9,5},... | collective-permute-start | bytes 1179656 | tf_op jit(solution)/shard_map/ppermute | solution.py:518

commit v2 on v1

--- a/solution.py
+++ b/solution.py
@@ -9,9 +9,9 @@
 
 SHARES = (1, 1)
 SET = 4
-BLOCKS = 4
+BLOCKS = 2
 VMEM_BYTES = 48 * 1024 * 1024
-PANELS_VMEM_BYTES = 56 * 1024 * 1024
+PANELS_VMEM_BYTES = 62 * 1024 * 1024
 WHOLE_VMEM_BYTES = 60 * 1024 * 1024
 SMEM = pl.BlockSpec(memory_space=pltpu.SMEM)
 HBM = pl.BlockSpec(memory_space=pltpu.HBM)
@@ -317,7 +317,7 @@
             pltpu.VMEM(other.shape, other.dtype),
             pltpu.SemaphoreType.DMA((2,)),
         ],
-        compiler_params=params(),
+        compiler_params=params(PANELS_VMEM_BYTES),
         name="left_pair",
     )(table, place, own, other)
 
@@ -342,7 +342,7 @@
         out_shape=jax.ShapeDtypeStruct(left.shape, left.dtype),
         in_specs=[VMEM, VMEM],
         out_specs=VMEM,
-        compiler_params=params(),
+        compiler_params=params(PANELS_VMEM_BYTES),
         name="product",
     )(left, right)
 
@@ -456,27 +456,29 @@
 
 def diagrams_kernel(whole_parts, table, place, *refs):
     wholes, rests = refs[:whole_parts], refs[whole_parts : 2 * whole_parts + 1]
-    pieces, (out, held) = refs[2 * whole_parts + 1 : -2], refs[-2:]
+    pieces, (out, held, lasts, sems) = refs[2 * whole_parts + 1 : -4], refs[-4:]
     mine = place[0] // SET
     for e, piece in enumerate(pieces):
         held[jnp.bitwise_xor(mine, e)] = piece[...]
 
     def write(wide):
         start = 0
-        for part, rest in zip([*wholes, held], rests):
+        for part in [*wholes, held]:
             width = part.shape[4]
+            columns = slice(start, start + width)
 
             def sum_at(code):
                 owner, slot = code // SET, lax.rem(code, SET)
                 if not wide:
                     return part[owner, slot].astype(jnp.float32)
                 usual = part[owner, jnp.minimum(slot, SET - 2)].astype(jnp.float32)
-                return jnp.where(slot == SET - 1, rest[owner, 0].astype(jnp.float32), usual)
+                last = lasts[owner, 0, :, :, columns].astype(jnp.float32)
+                return jnp.where(slot == SET - 1, last, usual)
 
             for d in range(out.shape[0]):
                 second = sum_at(jnp.maximum(table[5, d], 0))
                 total = sum_at(table[4, d]) + jnp.where(table[5, d] >= 0, second, 0.0)
-                out[d, :, :, start : start + width] = total.astype(out.dtype)
+                out[d, :, :, columns] = total.astype(out.dtype)
             start += width
 
     @pl.when(table[8, 0] < SET)
@@ -485,6 +487,17 @@
 
     @pl.when(table[8, 0] == SET)
     def _():
+        start, copies = 0, []
+        for j, rest in enumerate(rests):
+            columns = pl.ds(start, rest.shape[4])
+            start += rest.shape[4]
+            copies.append(
+                pltpu.make_async_copy(rest, lasts.at[:, :, :, :, columns], sems.at[j])
+            )
+        for copy in copies:
+            copy.start()
+        for copy in copies:
+            copy.wait()
         write(True)
 
 
@@ -496,9 +509,13 @@
     return pl.pallas_call(
         functools.partial(diagrams_kernel, len(wholes)),
         out_shape=jax.ShapeDtypeStruct((table.shape[1] // 2, two, rows, order), dtype),
-        in_specs=[SMEM, SMEM] + [VMEM] * len(operands),
+        in_specs=[SMEM, SMEM] + [VMEM] * len(wholes) + [HBM] * len(rests) + [VMEM] * len(pieces),
         out_specs=VMEM,
-        scratch_shapes=[pltpu.VMEM((len(pieces),) + pieces[0].shape, dtype)],
+        scratch_shapes=[
+            pltpu.VMEM((len(pieces),) + pieces[0].shape, dtype),
+            pltpu.VMEM((len(pieces), 1, two, rows, order), dtype),
+            pltpu.SemaphoreType.DMA((len(rests),)),
+        ],
         compiler_params=params(),
         name="diagrams",
     )(table, place, *operands)

time: 398 us -> 397 us (level)
  local copies, waits for them, and re-layouts: 11.6 us -> 6.1 us
    unnamed x23 -> x17, local copies, waits for them, and re-layouts: 11 us -> 5.57 us
  transfers between devices with their start and end apart: 18 -> 18, of which waited for: 15 -> 15; matrix products, arithmetic and copies ran while one was open for 0% -> 0% of each run, Pallas kernels for 15% -> 16%
where the time goes in v2:
time: 397 us
  waiting for transfers between devices  265 us (67%)
  Pallas kernels  78.7 us (20%)
  starting transfers between devices  45.5 us (11%)
  local copies, waits for them, and re-layouts  6.1 us (2%)
    ppermute x13, waiting for transfers between devices, swap(): return lax.ppermute(x, 'node', [(i, i ^ shift) for i in range(size)])  152 us
    all_to_all x5, waiting for transfers between devices, exchange(): lax.all_to_all(x, 'node', split_axis=0, concat_axis=0, axis_index_groups=...  113 us
    all_to_all x5, starting transfers between devices, exchange(): lax.all_to_all(x, 'node', split_axis=0, concat_axis=0, axis_index_groups=...  34.5 us
    pallas_call x2, Pallas kernels, panels_of(): pl.pallas_call(panels_kernel, out_shape=[jax.ShapeDtypeStruct((sets, two,...  17.2 us
    pallas_call x1, Pallas kernels, left_pair(): pl.pallas_call(left_kernel, out_shape=jax.ShapeDtypeStruct((2, order, ord...  16 us
    pallas_call x1, Pallas kernels, product(): pl.pallas_call(product_kernel, out_shape=jax.ShapeDtypeStruct(left.shape,...  14.3 us
    ppermute x13, starting transfers between devices, swap(): return lax.ppermute(x, 'node', [(i, i ^ shift) for i in range(size)])  11.1 us
    pallas_call x2, Pallas kernels, pick(): pl.pallas_call(functools.partial(pick_kernel, row, start), out_shape=jax....  10.2 us
  transfers between devices with their start and end apart: 18, of which 15 were waited for; matrix products, arithmetic and copies ran while one was open for 0% of the time, Pallas kernels for 16%

profile of v2, /device:TPU:10, one launch (start us, length us, event | category | flops | bytes accessed | tf_op | source)
XLA Modules:
  0.0 396.5 jit_solution(10435962195158828213)
XLA Ops:
  1.4 4.5 %route.1.table = s32[9,16]{1,0:T(8,128)} custom-call(s32[1]{0:T(128)} %bitcast.place_ref.place, s32[16,2]{1,0:T(8,128)} %copy.7.pair_nodes, s32[16]{0:T(128)} %prod_left.1, s32[16]{0:T(128)} %prod_right.1, s32[16]{0:T(128)} %prod_flag.1, s32[16]{0:T(128)} %prod_diag.1), custom_call_target="tpu_custom_call" | custom-call | tf_op jit(solution)/shard_map/route/pallas_call | solution.py:133
  5.8 5.1 %pick.2 = bf16[16,2,64,1024]{3,2,1,0:T(8,128)(2,1)} custom-call(s32[9,16]{1,0:T(8,128)} %route.1.table, bf16[64,2,64,1024]{3,2,1,0:T(8,128)(2,1)} %nodes.5), custom_call_target="tpu_custom_call" | custom-call | tf_op jit(solution)/shard_map/pick/pallas_call | solution.py:165
  11.0 6.3 %all-to-all-start.2 = ((bf16[16,2,64,1024]{3,2,1,0:T(8,128)(2,1)}), bf16[16,2,64,1024]{3,2,1,0:T(8,128)(2,1)}, u32[]{:S(2)}, u32[]{:S(2)}) async-start(bf16[16,2,64,1024]{3,2,1,0:T(8,128)(2,1)} %pick.2), calls=%async_computation.2 | async-start | bytes 8388608 | tf_op jit(solution)/shard_map/all_to_all | solution.py:525
  17.3 4.6 %pick_sets.1 = (bf16[4,2,64,1024]{3,2,1,0:T(8,128)(2,1)}, bf16[4,2,64,1024]{3,2,1,0:T(8,128)(2,1)}, bf16[4,2,64,1024]{3,2,1,0:T(8,128)(2,1)}, bf16[4,2,64,1024]{3,2,1,0:T(8,128)(2,1)}) custom-call(s32[1]{0:T(128)} %bitcast.place_ref.place, s32[9,16]{1,0:T(8,128)} %route.1.table, bf16[64,2,64,1024]{3,2,1,0:T(8,128)(2,1)} %nodes.5), custom_call_target="tpu_custom_call" | custom-call | tf_op jit(solution)/shard_map/pick_sets/pallas_call | solution.py:205
  23.5 5.0 %pick.3 = bf16[16,2,64,1024]{3,2,1,0:T(8,128)(2,1)} custom-call(s32[9,16]{1,0:T(8,128)} %route.1.table, bf16[64,2,64,1024]{3,2,1,0:T(8,128)(2,1)} %nodes.5), custom_call_target="tpu_custom_call" | custom-call | tf_op jit(solution)/shard_map/pick/pallas_call | solution.py:165
  28.5 43.1 %collective-permute-done.1.refs_2_ = bf16[4,2,64,1024]{3,2,1,0:T(8,128)(2,1)S(1)} collective-permute-done((bf16[4,2,64,1024]{3,2,1,0:T(8,128)(2,1)}, bf16[4,2,64,1024]{3,2,1,0:T(8,128)(2,1)S(1)}, u32[]{:S(2)}, u32[]{:S(2)}) %collective-permute-start.1) | collective-permute-done | bytes 1048608 | tf_op jit(solution)/shard_map/ppermute | solution.py:535
  71.6 36.6 %all-to-all-done.2.own = bf16[16,2,64,1024]{3,2,1,0:T(8,128)(2,1)} async-done(((bf16[16,2,64,1024]{3,2,1,0:T(8,128)(2,1)}), bf16[16,2,64,1024]{3,2,1,0:T(8,128)(2,1)}, u32[]{:S(2)}, u32[]{:S(2)}) %all-to-all-start.2) | async-done | bytes 4194336 | tf_op jit(solution)/shard_map/all_to_all | solution.py:525
  108.2 6.6 %all-to-all-start.3 = ((bf16[16,2,64,1024]{3,2,1,0:T(8,128)(2,1)}), bf16[16,2,64,1024]{3,2,1,0:T(8,128)(2,1)}, u32[]{:S(2)}, u32[]{:S(2)}) async-start(bf16[16,2,64,1024]{3,2,1,0:T(8,128)(2,1)} %pick.3), calls=%async_computation.3 | async-start | bytes 8388608 | tf_op jit(solution)/shard_map/all_to_all | solution.py:525
  116.5 7.2 %collective-permute-done.2.refs_1_ = bf16[4,2,64,1024]{3,2,1,0:T(8,128)(2,1)S(1)} collective-permute-done((bf16[4,2,64,1024]{3,2,1,0:T(8,128)(2,1)}, bf16[4,2,64,1024]{3,2,1,0:T(8,128)(2,1)S(1)}, u32[]{:S(2)}, u32[]{:S(2)}) %collective-permute-start.2) | collective-permute-done | bytes 1048608 | tf_op jit(solution)/shard_map/ppermute | solution.py:535
  123.7 44.9 %collective-permute-done.3.refs_3_ = bf16[4,2,64,1024]{3,2,1,0:T(8,128)(2,1)S(1)} collective-permute-done((bf16[4,2,64,1024]{3,2,1,0:T(8,128)(2,1)S(1)}, bf16[4,2,64,1024]{3,2,1,0:T(8,128)(2,1)S(1)}, u32[]{:S(2)}, u32[]{:S(2)}) %collective-permute-start.3) | collective-permute-done | bytes 1048608 | tf_op jit(solution)/shard_map/ppermute | solution.py:535
  169.6 4.0 %regroup.1 = (bf16[4,4,2,64,512]{4,3,2,1,0:T(8,128)(2,1)}, bf16[4,4,2,64,512]{4,3,2,1,0:T(8,128)(2,1)}) custom-call(bf16[4,2,64,1024]{3,2,1,0:T(8,128)(2,1)} %get-tuple-element.48.refs_0_, bf16[4,2,64,1024]{3,2,1,0:T(8,128)(2,1)} %copy-done.5, bf16[4,2,64,1024]{3,2,1,0:T(8,128)(2,1)} %copy-done.4, bf16[4,2,64,1024]{3,2,1,0:T(8,128)(2,1)} %copy-done.6), custom_call_target="tpu_custom_call" | custom-call | tf_op jit(solution)/shard_map/regroup/pallas_call | solution.py:247
  173.6 16.0 %left_pair.1.left = bf16[2,1024,1024]{2,1,0:T(8,128)(2,1)} custom-call(s32[9,16]{1,0:T(8,128)} %route.1.table, s32[1]{0:T(128)} %bitcast.place_ref.place, bf16[16,2,64,1024]{3,2,1,0:T(8,128)(2,1)} %all-to-all-done.2.own, bf16[16,2,64,1024]{3,2,1,0:T(8,128)(2,1)} %collective-permute-done.other), custom_call_target="tpu_custom_call" | custom-call | tf_op jit(solution)/shard_map/left_pair/pallas_call | solution.py:310
  189.5 16.2 %all-to-all-done.3.right = bf16[16,2,64,1024]{3,2,1,0:T(8,128)(2,1)} async-done(((bf16[16,2,64,1024]{3,2,1,0:T(8,128)(2,1)}), bf16[16,2,64,1024]{3,2,1,0:T(8,128)(2,1)}, u32[]{:S(2)}, u32[]{:S(2)}) %all-to-all-start.3) | async-done | bytes 4194336 | tf_op jit(solution)/shard_map/all_to_all | solution.py:525
  205.7 6.0 %all-to-all-start.4 = ((bf16[4,4,2,64,512]{4,3,2,1,0:T(8,128)(2,1)}), bf16[4,4,2,64,512]{4,3,2,1,0:T(8,128)(2,1)}, u32[]{:S(2)}, u32[]{:S(2)}) async-start(bf16[4,4,2,64,512]{4,3,2,1,0:T(8,128)(2,1)} %get-tuple-element.52), calls=%async_computation.4 | async-start | bytes 4194304 | tf_op jit(solution)/shard_map/all_to_all | solution.py:525
  211.7 14.3 %product.1.left_hbm = bf16[2,1024,1024]{2,1,0:T(8,128)(2,1)} custom-call(bf16[2,1024,1024]{2,1,0:T(8,128)(2,1)} %left_pair.1.left, bf16[16,2,64,1024]{3,2,1,0:T(8,128)(2,1)} %all-to-all-done.3.right), custom_call_target="tpu_custom_call" | custom-call | tf_op jit(solution)/shard_map/product/pallas_call | solution.py:340
  226.0 30.5 %all-to-all-done.4.right_hbm = bf16[4,4,2,64,512]{4,3,2,1,0:T(8,128)(2,1)} async-done(((bf16[4,4,2,64,512]{4,3,2,1,0:T(8,128)(2,1)}), bf16[4,4,2,64,512]{4,3,2,1,0:T(8,128)(2,1)}, u32[]{:S(2)}, u32[]{:S(2)}) %all-to-all-start.4) | async-done | bytes 2097184 | tf_op jit(solution)/shard_map/all_to_all | solution.py:525
  256.4 8.7 %all-to-all-start.6 = ((bf16[4,4,2,64,512]{4,3,2,1,0:T(8,128)(2,1)}), bf16[4,4,2,64,512]{4,3,2,1,0:T(8,128)(2,1)}, u32[]{:S(2)}, u32[]{:S(2)}) async-start(bf16[4,4,2,64,512]{4,3,2,1,0:T(8,128)(2,1)} %get-tuple-element.60), calls=%async_computation.6 | async-start | bytes 4194304 | tf_op jit(solution)/shard_map/all_to_all | solution.py:525
  265.1 8.6 %panels.2 = (bf16[4,2,64,512]{3,2,1,0:T(8,128)(2,1)}, bf16[4,2,64,512]{3,2,1,0:T(8,128)(2,1)}, bf16[4,2,64,512]{3,2,1,0:T(8,128)(2,1)}, bf16[4,2,64,512]{3,2,1,0:T(8,128)(2,1)}) custom-call(s32[1]{0:T(128)} %bitcast.place_ref.place, bf16[2,1024,1024]{2,1,0:T(8,128)(2,1)} %product.1.left_hbm, bf16[4,4,2,64,512]{4,3,2,1,0:T(8,128)(2,1)} %all-to-all-done.4.right_hbm), custom_call_target="tpu_custom_call" | custom-call | tf_op jit(solution)/shard_map/panels/pallas_call | solution.py:392
  275.9 12.9 %collective-permute-done.5.refs_2_ = bf16[4,2,64,512]{3,2,1,0:T(8,128)(2,1)S(1)} collective-permute-done((bf16[4,2,64,512]{3,2,1,0:T(8,128)(2,1)}, bf16[4,2,64,512]{3,2,1,0:T(8,128)(2,1)S(1)}, u32[]{:S(2)}, u32[]{:S(2)}) %collective-permute-start.5) | collective-permute-done | bytes 524320 | tf_op jit(solution)/shard_map/ppermute | solution.py:535
  288.8 10.3 %collective-permute-done.6.refs_3_ = bf16[4,2,64,512]{3,2,1,0:T(8,128)(2,1)S(1)} collective-permute-done((bf16[4,2,64,512]{3,2,1,0:T(8,128)(2,1)}, bf16[4,2,64,512]{3,2,1,0:T(8,128)(2,1)S(1)}, u32[]{:S(2)}, u32[]{:S(2)}) %collective-permute-start.6) | collective-permute-done | bytes 524320 | tf_op jit(solution)/shard_map/ppermute | solution.py:535
  300.1 2.3 sums.2
  303.6 7.0 %all-to-all-done.6.right_hbm = bf16[4,4,2,64,512]{4,3,2,1,0:T(8,128)(2,1)} async-done(((bf16[4,4,2,64,512]{4,3,2,1,0:T(8,128)(2,1)}), bf16[4,4,2,64,512]{4,3,2,1,0:T(8,128)(2,1)}, u32[]{:S(2)}, u32[]{:S(2)}) %all-to-all-start.6) | async-done | bytes 2097184 | tf_op jit(solution)/shard_map/all_to_all | solution.py:525
  310.5 6.9 %all-to-all-start.5 = ((bf16[4,3,2,64,512]{4,3,2,1,0:T(8,128)(2,1)}), bf16[4,3,2,64,512]{4,3,2,1,0:T(8,128)(2,1)S(1)}, u32[]{:S(2)}, u32[]{:S(2)}) async-start(bf16[4,3,2,64,512]{4,3,2,1,0:T(8,128)(2,1)} %copy-done), calls=%async_computation.5 | async-start | bytes 3145728 | tf_op jit(solution)/shard_map/all_to_all | solution.py:525
  317.4 8.6 %panels.3 = (bf16[4,2,64,512]{3,2,1,0:T(8,128)(2,1)}, bf16[4,2,64,512]{3,2,1,0:T(8,128)(2,1)}, bf16[4,2,64,512]{3,2,1,0:T(8,128)(2,1)}, bf16[4,2,64,512]{3,2,1,0:T(8,128)(2,1)}) custom-call(s32[1]{0:T(128)} %bitcast.place_ref.place, bf16[2,1024,1024]{2,1,0:T(8,128)(2,1)} %product.1.left_hbm, bf16[4,4,2,64,512]{4,3,2,1,0:T(8,128)(2,1)} %all-to-all-done.6.right_hbm), custom_call_target="tpu_custom_call" | custom-call | tf_op jit(solution)/shard_map/panels/pallas_call | solution.py:392
  326.2 1.8 collective-permute-start.9
  328.0 22.8 %all-to-all-done.5.refs_0_ = bf16[4,3,2,64,512]{4,3,2,1,0:T(8,128)(2,1)S(1)} async-done(((bf16[4,3,2,64,512]{4,3,2,1,0:T(8,128)(2,1)}), bf16[4,3,2,64,512]{4,3,2,1,0:T(8,128)(2,1)S(1)}, u32[]{:S(2)}, u32[]{:S(2)}) %all-to-all-start.5) | async-done | bytes 1572896 | tf_op jit(solution)/shard_map/all_to_all | solution.py:525
  352.6 3.0 sums.3
  355.6 2.5 collective-permute-start.10
  360.7 12.8 %collective-permute-done.10.refs_4_ = bf16[3,2,64,512]{3,2,1,0:T(8,128)(2,1)S(1)} collective-permute-done((bf16[3,2,64,512]{3,2,1,0:T(8,128)(2,1)}, bf16[3,2,64,512]{3,2,1,0:T(8,128)(2,1)S(1)}, u32[]{:S(2)}, u32[]{:S(2)}) %collective-permute-start.10) | collective-permute-done | bytes 393248 | tf_op jit(solution)/shard_map/ppermute | solution.py:535
  373.6 11.7 %collective-permute-done.11.refs_5_ = bf16[3,2,64,512]{3,2,1,0:T(8,128)(2,1)S(1)} collective-permute-done((bf16[3,2,64,512]{3,2,1,0:T(8,128)(2,1)}, bf16[3,2,64,512]{3,2,1,0:T(8,128)(2,1)S(1)}, u32[]{:S(2)}, u32[]{:S(2)}) %collective-permute-start.11) | collective-permute-done | bytes 393248 | tf_op jit(solution)/shard_map/ppermute | solution.py:535
  385.2 8.4 %collective-permute-done.12.refs_6_ = bf16[3,2,64,512]{3,2,1,0:T(8,128)(2,1)S(1)} collective-permute-done((bf16[3,2,64,512]{3,2,1,0:T(8,128)(2,1)}, bf16[3,2,64,512]{3,2,1,0:T(8,128)(2,1)S(1)}, u32[]{:S(2)}, u32[]{:S(2)}) %collective-permute-start.12) | collective-permute-done | bytes 393248 | tf_op jit(solution)/shard_map/ppermute | solution.py:535
  393.6 2.7 diagrams.1
  (35 shorter events, 14.0 us)
Async XLA Ops:
  11.0 97.2 %all-to-all-start.2 = ((bf16[16,2,64,1024]{3,2,1,0:T(8,128)(2,1)}), bf16[16,2,64,1024]{3,2,1,0:T(8,128)(2,1)}, u32[]{:S(2)}, u32[]{:S(2)}) async-start(bf16[16,2,64,1024]{3,2,1,0:T(8,128)(2,1)} %pick.2), calls=%async_computation.2 | async-start | bytes 8388608 | tf_op jit(solution)/shard_map/all_to_all | solution.py:525
  22.0 49.6 %collective-permute-start.1 = (bf16[4,2,64,1024]{3,2,1,0:T(8,128)(2,1)}, bf16[4,2,64,1024]{3,2,1,0:T(8,128)(2,1)S(1)}, u32[]{:S(2)}, u32[]{:S(2)}) collective-permute-start(bf16[4,2,64,1024]{3,2,1,0:T(8,128)(2,1)} %get-tuple-element.46), channel_id=1, source_target_pairs={{0,2},{1,3},{2,0},{3,1},{4,6},{5,7},{6,4},{7,5},{8,10},{9,11},{10,... | collective-permute-start | bytes 3145736 | tf_op jit(solution)/shard_map/ppermute | solution.py:535
  28.5 86.8 %copy-start.7 = (bf16[4,2,64,1024]{3,2,1,0:T(8,128)(2,1)S(1)}, bf16[4,2,64,1024]{3,2,1,0:T(8,128)(2,1)}, u32[]{:S(2)}) copy-start(bf16[4,2,64,1024]{3,2,1,0:T(8,128)(2,1)} %get-tuple-element.50) | copy-start | bytes 3145732
  71.6 36.6 %copy-start.4 = (bf16[4,2,64,1024]{3,2,1,0:T(8,128)(2,1)}, bf16[4,2,64,1024]{3,2,1,0:T(8,128)(2,1)S(1)}, u32[]{:S(2)}) copy-start(bf16[4,2,64,1024]{3,2,1,0:T(8,128)(2,1)S(1)} %collective-permute-done.1.refs_2_) | copy-start | bytes 3145732
  108.2 97.5 %all-to-all-start.3 = ((bf16[16,2,64,1024]{3,2,1,0:T(8,128)(2,1)}), bf16[16,2,64,1024]{3,2,1,0:T(8,128)(2,1)}, u32[]{:S(2)}, u32[]{:S(2)}) async-start(bf16[16,2,64,1024]{3,2,1,0:T(8,128)(2,1)} %pick.3), calls=%async_computation.3 | async-start | bytes 8388608 | tf_op jit(solution)/shard_map/all_to_all | solution.py:525
  114.8 58.8 %collective-permute-start = (bf16[16,2,64,1024]{3,2,1,0:T(8,128)(2,1)}, bf16[16,2,64,1024]{3,2,1,0:T(8,128)(2,1)}, u32[]{:S(2)}, u32[]{:S(2)}) collective-permute-start(bf16[16,2,64,1024]{3,2,1,0:T(8,128)(2,1)} %all-to-all-done.2.own), channel_id=1, source_target_pairs={{0,1},{1,0},{2,3},{3,2},{4,5},{5,4},{6,7},{7,6},{8,9},{9,8},{10,11... | collective-permute-start | bytes 12582920 | tf_op jit(solution)/shard_map/ppermute | solution.py:535
  114.9 8.7 %collective-permute-start.2 = (bf16[4,2,64,1024]{3,2,1,0:T(8,128)(2,1)}, bf16[4,2,64,1024]{3,2,1,0:T(8,128)(2,1)S(1)}, u32[]{:S(2)}, u32[]{:S(2)}) collective-permute-start(bf16[4,2,64,1024]{3,2,1,0:T(8,128)(2,1)} %get-tuple-element.49), channel_id=1, source_target_pairs={{0,1},{1,0},{2,3},{3,2},{4,5},{5,4},{6,7},{7,6},{8,9},{9,8},{10,11... | collective-permute-start | bytes 3145736 | tf_op jit(solution)/shard_map/ppermute | solution.py:535
  115.3 53.3 %collective-permute-start.3 = (bf16[4,2,64,1024]{3,2,1,0:T(8,128)(2,1)S(1)}, bf16[4,2,64,1024]{3,2,1,0:T(8,128)(2,1)S(1)}, u32[]{:S(2)}, u32[]{:S(2)}) collective-permute-start(bf16[4,2,64,1024]{3,2,1,0:T(8,128)(2,1)S(1)} %copy-done.7), channel_id=1, source_target_pairs={{0,3},{1,2},{2,1},{3,0},{4,7},{5,6},{6,5},{7,4},{8,11},{9,10},{10,... | collective-permute-start | bytes 3145736 | tf_op jit(solution)/shard_map/ppermute | solution.py:535
  123.7 44.9 %copy-start.5 = (bf16[4,2,64,1024]{3,2,1,0:T(8,128)(2,1)}, bf16[4,2,64,1024]{3,2,1,0:T(8,128)(2,1)S(1)}, u32[]{:S(2)}) copy-start(bf16[4,2,64,1024]{3,2,1,0:T(8,128)(2,1)S(1)} %collective-permute-done.2.refs_1_) | copy-start | bytes 3145732
  168.6 1.0 copy-start.6
  205.7 50.8 %all-to-all-start.4 = ((bf16[4,4,2,64,512]{4,3,2,1,0:T(8,128)(2,1)}), bf16[4,4,2,64,512]{4,3,2,1,0:T(8,128)(2,1)}, u32[]{:S(2)}, u32[]{:S(2)}) async-start(bf16[4,4,2,64,512]{4,3,2,1,0:T(8,128)(2,1)} %get-tuple-element.52), calls=%async_computation.4 | async-start | bytes 4194304 | tf_op jit(solution)/shard_map/all_to_all | solution.py:525
  256.4 54.1 %all-to-all-start.6 = ((bf16[4,4,2,64,512]{4,3,2,1,0:T(8,128)(2,1)}), bf16[4,4,2,64,512]{4,3,2,1,0:T(8,128)(2,1)}, u32[]{:S(2)}, u32[]{:S(2)}) async-start(bf16[4,4,2,64,512]{4,3,2,1,0:T(8,128)(2,1)} %get-tuple-element.60), calls=%async_computation.6 | async-start | bytes 4194304 | tf_op jit(solution)/shard_map/all_to_all | solution.py:525
  265.1 34.0 %copy-start.3 = (s32[9,16]{1,0:T(8,128)S(1)}, s32[9,16]{1,0:T(8,128)}, u32[]{:S(2)}) copy-start(s32[9,16]{1,0:T(8,128)} %route.1.table) | copy-start | bytes 1732
  273.7 2.2 collective-permute-start.4
  273.8 15.0 %collective-permute-start.5 = (bf16[4,2,64,512]{3,2,1,0:T(8,128)(2,1)}, bf16[4,2,64,512]{3,2,1,0:T(8,128)(2,1)S(1)}, u32[]{:S(2)}, u32[]{:S(2)}) collective-permute-start(bf16[4,2,64,512]{3,2,1,0:T(8,128)(2,1)} %get-tuple-element.55), channel_id=1, source_target_pairs={{0,2},{1,3},{2,0},{3,1},{4,6},{5,7},{6,4},{7,5},{8,10},{9,11},{10,... | collective-permute-start | bytes 1572872 | tf_op jit(solution)/shard_map/ppermute | solution.py:535
  274.7 24.4 %collective-permute-start.6 = (bf16[4,2,64,512]{3,2,1,0:T(8,128)(2,1)}, bf16[4,2,64,512]{3,2,1,0:T(8,128)(2,1)S(1)}, u32[]{:S(2)}, u32[]{:S(2)}) collective-permute-start(bf16[4,2,64,512]{3,2,1,0:T(8,128)(2,1)} %get-tuple-element.56), channel_id=1, source_target_pairs={{0,3},{1,2},{2,1},{3,0},{4,7},{5,6},{6,5},{7,4},{8,11},{9,10},{10,... | collective-permute-start | bytes 1572872 | tf_op jit(solution)/shard_map/ppermute | solution.py:535
  299.1 1.0 copy-start.2
  302.4 1.1 copy-start
  310.5 40.2 %all-to-all-start.5 = ((bf16[4,3,2,64,512]{4,3,2,1,0:T(8,128)(2,1)}), bf16[4,3,2,64,512]{4,3,2,1,0:T(8,128)(2,1)S(1)}, u32[]{:S(2)}, u32[]{:S(2)}) async-start(bf16[4,3,2,64,512]{4,3,2,1,0:T(8,128)(2,1)} %copy-done), calls=%async_computation.5 | async-start | bytes 3145728 | tf_op jit(solution)/shard_map/all_to_all | solution.py:525
  326.0 24.7 %collective-permute-start.7 = (bf16[4,2,64,512]{3,2,1,0:T(8,128)(2,1)}, bf16[4,2,64,512]{3,2,1,0:T(8,128)(2,1)S(1)}, u32[]{:S(2)}, u32[]{:S(2)}) collective-permute-start(bf16[4,2,64,512]{3,2,1,0:T(8,128)(2,1)} %get-tuple-element.63), channel_id=1, source_target_pairs={{0,1},{1,0},{2,3},{3,2},{4,5},{5,4},{6,7},{7,6},{8,9},{9,8},{10,11... | collective-permute-start | bytes 1572872 | tf_op jit(solution)/shard_map/ppermute | solution.py:535
  326.1 24.6 %collective-permute-start.8 = (bf16[4,2,64,512]{3,2,1,0:T(8,128)(2,1)}, bf16[4,2,64,512]{3,2,1,0:T(8,128)(2,1)S(1)}, u32[]{:S(2)}, u32[]{:S(2)}) collective-permute-start(bf16[4,2,64,512]{3,2,1,0:T(8,128)(2,1)} %get-tuple-element.64), channel_id=1, source_target_pairs={{0,2},{1,3},{2,0},{3,1},{4,6},{5,7},{6,4},{7,5},{8,10},{9,11},{10,... | collective-permute-start | bytes 1572872 | tf_op jit(solution)/shard_map/ppermute | solution.py:535
  326.2 25.4 %collective-permute-start.9 = (bf16[4,2,64,512]{3,2,1,0:T(8,128)(2,1)}, bf16[4,2,64,512]{3,2,1,0:T(8,128)(2,1)}, u32[]{:S(2)}, u32[]{:S(2)}) collective-permute-start(bf16[4,2,64,512]{3,2,1,0:T(8,128)(2,1)} %get-tuple-element.65), channel_id=1, source_target_pairs={{0,3},{1,2},{2,1},{3,0},{4,7},{5,6},{6,5},{7,4},{8,11},{9,10},{10,... | collective-permute-start | bytes 1572872 | tf_op jit(solution)/shard_map/ppermute | solution.py:535
  351.6 1.0 copy-start.1
  355.6 18.0 %collective-permute-start.10 = (bf16[3,2,64,512]{3,2,1,0:T(8,128)(2,1)}, bf16[3,2,64,512]{3,2,1,0:T(8,128)(2,1)S(1)}, u32[]{:S(2)}, u32[]{:S(2)}) collective-permute-start(bf16[3,2,64,512]{3,2,1,0:T(8,128)(2,1)} %get-tuple-element.74), channel_id=1, source_target_pairs={{0,4},{1,5},{2,6},{3,7},{4,0},{5,1},{6,2},{7,3},{8,12},{9,13},{10,... | collective-permute-start | bytes 1179656 | tf_op jit(solution)/shard_map/ppermute | solution.py:535
  358.1 27.2 %collective-permute-start.11 = (bf16[3,2,64,512]{3,2,1,0:T(8,128)(2,1)}, bf16[3,2,64,512]{3,2,1,0:T(8,128)(2,1)S(1)}, u32[]{:S(2)}, u32[]{:S(2)}) collective-permute-start(bf16[3,2,64,512]{3,2,1,0:T(8,128)(2,1)} %get-tuple-element.75), channel_id=1, source_target_pairs={{0,8},{1,9},{2,10},{3,11},{4,12},{5,13},{6,14},{7,15},{8,0},{9,1},... | collective-permute-start | bytes 1179656 | tf_op jit(solution)/shard_map/ppermute | solution.py:535
  358.5 35.1 %collective-permute-start.12 = (bf16[3,2,64,512]{3,2,1,0:T(8,128)(2,1)}, bf16[3,2,64,512]{3,2,1,0:T(8,128)(2,1)S(1)}, u32[]{:S(2)}, u32[]{:S(2)}) collective-permute-start(bf16[3,2,64,512]{3,2,1,0:T(8,128)(2,1)} %get-tuple-element.76), channel_id=1, source_target_pairs={{0,12},{1,13},{2,14},{3,15},{4,8},{5,9},{6,10},{7,11},{8,4},{9,5},... | collective-permute-start | bytes 1179656 | tf_op jit(solution)/shard_map/ppermute | solution.py:535
